TPU v7x, 256 devices: a whole 4x4x8 slice. The times are simulated.
256 devices in a mesh: shot: 32 (over x, y, core), xline: 8 (over z).
Axes of the slice: x: 4, y: 4, z: 8, core: 2. Of those that a mesh axis runs over, the one named last changes fastest.
Arguments:
- records: bfloat16 [64, 512, 2048], P('shot', 'xline'), may hold values from -2 to 2
- source_trace: int32 [32, 32, 16], replicated, may hold values from 0 to 127
- target_trace: int32 [32, 32, 16], P('shot'), may hold values from 0 to 1
- mirror: int32 [32, 32, 16], P('shot'), may hold values from 0 to 511
- live_slots: int32 [32, 32], P('shot'), may hold values from 4 to 16, as said below
Outputs:
- predicted: float32 [64, 512, 2048], P('shot', 'xline')
Inputs may be any that keep to these rules, and one draw needn't show every extreme that they name: live_slots[d, d] = 16 for every owner d, and one owner has 16 live slots from every owner.
All inputs are finite; a program needn't handle non-finite values.
Results may differ from a plain program's by a relative error of at most 0.0064.
Values may be sent and summed in bfloat16 or wider, within the bound.
No kernel may reach another device: no remote copies, remote signals or barrier semaphores. Data moves between devices by JAX's collectives and lax.ppermute only.
A program may use at most 128 MiB of HBM per device.

v0:
```python
import math

import jax
import jax.numpy as jnp
from jax import lax
from jax.sharding import PartitionSpec as P


def tables(length):
    spectral = length // 2
    times_col = jnp.arange(length, dtype=jnp.int32)[:, None]
    freq_row = jnp.arange(spectral, dtype=jnp.int32)[None, :]
    phases = (times_col * freq_row % length).astype(jnp.float32) * (2.0 * math.pi / length)
    cos_part = jnp.cos(phases)
    sin_part = jnp.sin(phases)
    forward_full = jnp.concatenate([cos_part, -sin_part], axis=1)
    weights = jnp.where(freq_row == 0, 1.0, 2.0).astype(jnp.float32) / length
    inverse_full = jnp.concatenate([(cos_part * weights).T, (-sin_part * weights).T], axis=0)
    return (forward_full.astype(jnp.bfloat16), inverse_full.astype(jnp.bfloat16))


def complex_product(left, right):
    spectral = left.shape[-1] // 2
    left = left.astype(jnp.float32)
    right = right.astype(jnp.float32)
    left_re, left_im = (left[:, :spectral], left[:, spectral:])
    right_re, right_im = (right[:, :spectral], right[:, spectral:])
    return jnp.concatenate(
        [left_re * right_re - left_im * right_im, left_re * right_im + left_im * right_re], axis=1
    )


def on_device(records, source_trace, target_trace, mirror, live_slots):
    shot_dev, rx_local, length = records.shape
    xlines = lax.axis_size("xline")
    recv_all = rx_local * xlines
    my_owner = lax.axis_index("shot")
    forward, inverse = tables(length)

    def transform(block_rows):
        return jnp.dot(block_rows, forward, preferred_element_type=jnp.float32).astype(jnp.bfloat16)

    own_spec = transform(records)
    spec_full = lax.all_gather(own_spec, "xline", axis=1, tiled=True)
    send_index = lax.dynamic_index_in_dim(source_trace, my_owner, 1, False)
    outgoing = records.reshape(shot_dev * rx_local, length)[send_index]
    received = transform(lax.all_to_all(outgoing, "shot", split_axis=0, concat_axis=0, tiled=True))
    my_source = lax.dynamic_index_in_dim(source_trace, my_owner, 0, False)
    r_local = my_source % rx_local
    targets = target_trace[0]
    mirrors = mirror[0]
    counts = live_slots[0]
    slot_ids = jnp.arange(my_source.shape[1], dtype=jnp.int32)[None, :]
    usable = (slot_ids < counts[:, None]).astype(jnp.float32).reshape(-1)
    a_rows = spec_full.reshape(shot_dev * recv_all, length)[
        (targets * recv_all + mirrors).reshape(-1)
    ]
    b_rows = received.reshape(-1, length)
    product = complex_product(a_rows, b_rows) * usable[:, None]
    out_index = (targets * rx_local + r_local).reshape(-1)
    onehot = (
        jnp.arange(shot_dev * rx_local, dtype=jnp.int32)[:, None] == out_index[None, :]
    ).astype(jnp.float32)
    summed = jnp.dot(
        onehot, product, precision=lax.Precision.HIGHEST, preferred_element_type=jnp.float32
    )
    predicted = jnp.dot(summed.astype(jnp.bfloat16), inverse, preferred_element_type=jnp.float32)
    return predicted.reshape(shot_dev, rx_local, length)


def solution(mesh):
    placed = (
        P("shot", "xline", None),
        P(),
        P("shot", None, None),
        P("shot", None, None),
        P("shot", None),
    )
    return jax.shard_map(
        on_device, mesh=mesh, in_specs=placed, out_specs=P("shot", "xline", None), check_vma=False
    )
```

profile of v0, /device:TPU:2, one launch (start us, length us, event | category | flops | bytes accessed | tf_op | source)
XLA Modules:
  0.0 126.3 jit_solution(15033789831118512977)
XLA Ops:
  6.5 33.8 %negate_convert_fusion = (bf16[2048,1024]{1,0:T(8,128)(2,1)S(1)}, bf16[2048,1024]{1,0:T(8,128)(2,1)S(1)}) fusion(), kind=kLoop, calls=%fused_computation.23 | loop fusion | flops 35651584 | bytes 8388608 | tf_op jit(solution)/shard_map/convert.5
  40.4 1.9 %copy-done.2 = bf16[2048,1024]{1,0:T(8,128)(2,1)} copy-done((bf16[2048,1024]{1,0:T(8,128)(2,1)}, bf16[2048,1024]{1,0:T(8,128)(2,1)S(1)}, u32[]{:S(2)}) %copy-start.2) | copy-done | bytes 4194328
  42.3 1.3 %copy-done.3 = bf16[2048,1024]{1,0:T(8,128)(2,1)} copy-done((bf16[2048,1024]{1,0:T(8,128)(2,1)}, bf16[2048,1024]{1,0:T(8,128)(2,1)S(1)}, u32[]{:S(2)}) %copy-start.3) | copy-done | bytes 4194328
  43.6 2.1 %fusion.24 = bf16[2,64,2048]{2,1,0:T(8,128)(2,1)} fusion(bf16[2,64,2048]{2,1,0:T(8,128)(2,1)S(1)} %copy-done, bf16[2048,1024]{1,0:T(8,128)(2,1)S(1)} %get-tuple-element.11, bf16[2048,1024]{1,0:T(8,128)(2,1)S(1)} %get-tuple-element.12), kind=kOutput, calls=%fused_computation.38 | convolution fusion | flops 1090781184 | bytes 9437184 | tf_op jit(solution)/shard_map/dot_general | solution.py:41
  45.7 0.1 constant_dynamic-slice_fusion
  45.8 0.2 copy.11
  46.0 0.1 copy.10
  46.1 0.1 reshape.146
  46.2 3.3 %gather_fusion.1 = bf16[512,2048]{1,0:T(8,128)(2,1)} fusion(bf16[128,2048]{1,0:T(8,128)(2,1)S(1)} %bitcast.28, s32[1024]{0:T(1024)S(1)} %pad_clamp_fusion), kind=kCustom, calls=%fused_computation.1 | custom fusion | bytes 4196352 | tf_op jit(solution)/shard_map/gather | solution.py:46
  49.5 7.8 %all-to-all-start = ((bf16[32,16,2048]{2,1,0:T(8,128)(2,1)}), bf16[32,16,2048]{2,1,0:T(8,128)(2,1)S(1)}, u32[]{:S(2)}, u32[]{:S(2)}) async-start(bf16[32,16,2048]{2,1,0:T(8,128)(2,1)} %bitcast.6), calls=%async_computation | async-start | bytes 4194304 | tf_op jit(solution)/shard_map/all_to_all | solution.py:47
  57.4 0.1 add.85
  57.6 0.1 squeeze.10
  57.7 0.1 mul.119
  57.9 0.1 reshape.135
  58.0 35.4 %multiply_convert_fusion.1 = (bf16[1024,2048]{1,0:T(8,128)(2,1)}, bf16[1024,2048]{1,0:T(8,128)(2,1)}) fusion(f32[1024]{0:T(1024)S(1)} %select_multiply_fusion), kind=kLoop, calls=%fused_computation.20 | loop fusion | flops 39845888 | bytes 8392704 | tf_op jit(solution)/shard_map/convert.2
  93.4 8.1 %fusion.21 = bf16[32,16,2048]{2,1,0:T(8,128)(2,1)S(1)} fusion(bf16[32,16,2048]{2,1,0:T(8,128)(2,1)S(1)} %all-to-all-done, bf16[2048,1024]{1,0:T(8,128)(2,1)} %copy-done.2, bf16[2048,1024]{1,0:T(8,128)(2,1)} %copy-done.3), kind=kOutput, calls=%fused_computation.35 | convolution fusion | flops 4312793088 | bytes 12582912 | tf_op jit(solution)/shard_map/dot_general | solution.py:41
  101.5 2.6 %bitcast_convert_fusion = f32[512,2048]{1,0:T(8,128)} fusion(bf16[32,16,2048]{2,1,0:T(8,128)(2,1)S(1)} %fusion.21), kind=kLoop, calls=%fused_computation.39 | loop fusion | flops 1048576 | bytes 6291456 | tf_op jit(solution)/shard_map/convert_element_type | solution.py:25
  104.1 7.1 %gather_fusion = bf16[512,2048]{1,0:T(8,128)(2,1)S(1)} fusion(bf16[1024,2048]{1,0:T(8,128)(2,1)} %bitcast.29, s32[1024]{0:T(1024)S(1)} %pad_clamp_fusion.1), kind=kCustom, calls=%fused_computation | custom fusion | bytes 4196352 | tf_op jit(solution)/shard_map/gather | solution.py:55
  111.2 0.5 convert_element_type.48
  111.8 1.7 %copy-done.1 = f32[512,2048]{1,0:T(8,128)S(1)} copy-done((f32[512,2048]{1,0:T(8,128)S(1)}, f32[512,2048]{1,0:T(8,128)}, u32[]{:S(2)}) %copy-start.1) | copy-done | bytes 4194328
  113.4 1.4 %multiply_subtract_fusion = (f32[512,1024]{1,0:T(8,128)S(1)}, f32[512,1024]{1,0:T(8,128)S(1)}) fusion(f32[512,2048]{1,0:T(8,128)S(1)} %copy-done.1, f32[512,2048]{1,0:T(8,128)S(1)} %convert_element_type.48), kind=kLoop, calls=%fused_computation.42 | loop fusion | flops 3145728 | bytes 12582912 | tf_op jit(solution)/shard_map/sub | solution.py:29
  114.9 1.9 %fusion.22 = bf16[128,2048]{1,0:T(8,128)(2,1)S(1)} fusion(f32[512,1024]{1,0:T(8,128)S(1)} %get-tuple-element.6, f32[512,1024]{1,0:T(8,128)S(1)} %get-tuple-element.5, f32[512]{0:T(512)S(1)} %reshape.135, s32[512]{0:T(512)S(1)} %fusion.29), kind=kOutput, calls=%fused_computation.36 | convolution fusion | flops 1613037568 | bytes 4722688 | tf_op jit(solution)/shard_map/dot_general | solution.py:64
  116.8 0.4 copy-done.4
  117.2 2.2 %fusion.6 = f32[128,2048]{1,0:T(8,128)} fusion(bf16[128,2048]{1,0:T(8,128)(2,1)S(1)} %fusion.22, bf16[1024,2048]{1,0:T(8,128)(2,1)S(1)} %copy-done.5, bf16[1024,2048]{1,0:T(8,128)(2,1)S(1)} %copy-done.4), kind=kOutput, calls=%fused_computation.15 | convolution fusion | flops 1090519040 | bytes 9961472 | tf_op jit(solution)/shard_map/dot_general | solution.py:67
  (32 shorter events, 0.4 us)
Async XLA Ops:
  6.5 37.1 %copy-start = (bf16[2,64,2048]{2,1,0:T(8,128)(2,1)S(1)}, bf16[2,64,2048]{2,1,0:T(8,128)(2,1)}, u32[]{:S(2)}) copy-start(bf16[2,64,2048]{2,1,0:T(8,128)(2,1)} %param.5) | copy-start | bytes 1572868
  6.5 97.5 %all-gather.2.cloned.1.call-start = ((), (), s32[]{:S(2)}) async-start(), calls=%async_computation.1 | async-start | bytes 4718592 | tf_op jit(solution)/shard_map/all_gather | solution.py:44
  40.4 1.9 %copy-start.2 = (bf16[2048,1024]{1,0:T(8,128)(2,1)}, bf16[2048,1024]{1,0:T(8,128)(2,1)S(1)}, u32[]{:S(2)}) copy-start(bf16[2048,1024]{1,0:T(8,128)(2,1)S(1)} %get-tuple-element.11) | copy-start | bytes 12582916
  40.4 3.2 %copy-start.3 = (bf16[2048,1024]{1,0:T(8,128)(2,1)}, bf16[2048,1024]{1,0:T(8,128)(2,1)S(1)}, u32[]{:S(2)}) copy-start(bf16[2048,1024]{1,0:T(8,128)(2,1)S(1)} %get-tuple-element.12) | copy-start | bytes 12582916
  43.6 2.1 %copy-start.6 = (s32[32,32,16]{1,2,0:T(8,128)S(1)}, s32[32,32,16]{1,2,0:T(8,128)}, u32[]{:S(2)}) copy-start(s32[32,32,16]{1,2,0:T(8,128)} %param.6) | copy-start | bytes 196612
  49.5 7.8 %copy-start.7 = (s32[1,32,16]{1,2,0:T(8,128)S(1)}, s32[1,32,16]{1,2,0:T(8,128)}, u32[]{:S(2)}) copy-start(s32[1,32,16]{1,2,0:T(8,128)} %param.7) | copy-start | bytes 6148
  49.5 7.8 %copy-start.8 = (s32[1,32,16]{1,2,0:T(8,128)S(1)}, s32[1,32,16]{1,2,0:T(8,128)}, u32[]{:S(2)}) copy-start(s32[1,32,16]{1,2,0:T(8,128)} %param.8) | copy-start | bytes 6148
  49.5 8.3 %copy-start.9 = (s32[1,32]{1,0:T(1,128)S(1)}, s32[1,32]{1,0:T(1,128)}, u32[]{:S(2)}) copy-start(s32[1,32]{1,0:T(1,128)} %param.9) | copy-start | bytes 388
  49.5 43.9 %all-to-all-start = ((bf16[32,16,2048]{2,1,0:T(8,128)(2,1)}), bf16[32,16,2048]{2,1,0:T(8,128)(2,1)S(1)}, u32[]{:S(2)}, u32[]{:S(2)}) async-start(bf16[32,16,2048]{2,1,0:T(8,128)(2,1)} %bitcast.6), calls=%async_computation | async-start | bytes 4194304 | tf_op jit(solution)/shard_map/all_to_all | solution.py:47
  111.2 2.2 %copy-start.1 = (f32[512,2048]{1,0:T(8,128)S(1)}, f32[512,2048]{1,0:T(8,128)}, u32[]{:S(2)}) copy-start(f32[512,2048]{1,0:T(8,128)} %bitcast_convert_fusion) | copy-start | bytes 12582916
  113.4 3.4 %copy-start.5 = (bf16[1024,2048]{1,0:T(8,128)(2,1)S(1)}, bf16[1024,2048]{1,0:T(8,128)(2,1)}, u32[]{:S(2)}) copy-start(bf16[1024,2048]{1,0:T(8,128)(2,1)} %get-tuple-element.10) | copy-start | bytes 12582916
  114.9 2.4 %copy-start.4 = (bf16[1024,2048]{1,0:T(8,128)(2,1)S(1)}, bf16[1024,2048]{1,0:T(8,128)(2,1)}, u32[]{:S(2)}) copy-start(bf16[1024,2048]{1,0:T(8,128)(2,1)} %get-tuple-element.9) | copy-start | bytes 12582916
Sparse Core Ops, SparseCore 0:
  45.8 57.7 all-gather.1
where the time goes:
time: 128 us; the launch traced here: 126 us
  other arithmetic  73.9 us (58%)
  local copies, waits for them, and re-layouts  16.8 us (13%)
  matrix products  14.3 us (11%)
  between operations  13.6 us (11%)
  starting transfers between devices  7.77 us (6%)
    another operation x2, other arithmetic  69.2 us
    dot_general x2, matrix products, transform(): jnp.dot(block_rows, forward, preferred_element_type=jnp.float32)  10.1 us
    all_to_all x1, starting transfers between devices, on_device(): lax.all_to_all(outgoing, 'shot', split_axis=0, concat_axis=0, tiled=True)  7.77 us
    gather x1, local copies, waits for them, and re-layouts, on_device(): spec_full.reshape(shot_dev * recv_all, length)  7.13 us
    unnamed x21, local copies, waits for them, and re-layouts  5.47 us
    gather x1, local copies, waits for them, and re-layouts, on_device(): outgoing = records.reshape(shot_dev * rx_local, length)[send_index]  3.33 us
    convert_element_type x1, other arithmetic, complex_product(): right = right.astype(jnp.float32)  2.59 us
  transfers between devices with their start and end apart: 2, of which 0 were waited for; matrix products, arithmetic and copies ran while one was open for 40% of the time, Pallas kernels for 0%

commit v1 on v0

v1 whole, which is shorter than its diff:
```python
import functools
import math

import jax
import jax.numpy as jnp
import numpy as np
from jax import lax
from jax.experimental import pallas as pl
from jax.experimental.pallas import tpu as pltpu
from jax.sharding import PartitionSpec as P

VMEM_LIMIT = 48 * 1024 * 1024
TILE = 256


def forward_table(length):
    spectral = length // 2
    t = np.arange(length, dtype=np.int64)[:, None]
    f = np.arange(spectral, dtype=np.int64)[None, :]
    phase = (t * f % length).astype(np.float64) * (2.0 * math.pi / length)
    return np.concatenate([np.cos(phase), -np.sin(phase)], axis=1).astype(jnp.bfloat16)


def transform_kernel(send_ref, rec_ref, table_ref, spec_ref, out_ref, pick):
    @pl.when(pl.program_id(0) == 0)
    def _():
        rows = lax.broadcasted_iota(jnp.int32, pick.shape, 1)
        pick[...] = (rows == send_ref[...]).astype(jnp.float32).astype(jnp.bfloat16)

    spec = jnp.dot(rec_ref[...], table_ref[...], preferred_element_type=jnp.float32).astype(jnp.bfloat16)
    spec_ref[...] = spec
    out_ref[...] = jnp.dot(pick[...], spec, preferred_element_type=jnp.float32).astype(jnp.bfloat16)


def transform(records, send, table):
    rows, length = records.shape
    entries = send.shape[0]
    whole = lambda j: (0, 0)
    cols = lambda j: (0, j)
    return pl.pallas_call(
        transform_kernel,
        grid=(length // TILE,),
        in_specs=[
            pl.BlockSpec((entries, 1), whole),
            pl.BlockSpec((rows, length), whole),
            pl.BlockSpec((length, TILE), cols),
        ],
        out_specs=[pl.BlockSpec((rows, TILE), cols), pl.BlockSpec((entries, TILE), cols)],
        out_shape=[
            jax.ShapeDtypeStruct((rows, length), jnp.bfloat16),
            jax.ShapeDtypeStruct((entries, length), jnp.bfloat16),
        ],
        scratch_shapes=[pltpu.VMEM((entries, rows), jnp.bfloat16)],
        compiler_params=pltpu.CompilerParams(vmem_limit_bytes=VMEM_LIMIT),
    )(send, records, table)


def predict_kernel(
    a_idx_ref, o_idx_ref, sre_ref, sim_ref, bre_ref, bim_ref, tre_ref, tim_ref, out_ref, pick, put
):
    step = pl.program_id(0)
    f32 = jnp.float32

    @pl.when(step == 0)
    def _():
        rows = lax.broadcasted_iota(jnp.int32, pick.shape, 1)
        pick[...] = (rows == a_idx_ref[...]).astype(f32).astype(jnp.bfloat16)
        dest = lax.broadcasted_iota(jnp.int32, put.shape, 0)
        put[...] = (dest == o_idx_ref[...]).astype(f32).astype(jnp.bfloat16)

    a_re = jnp.dot(pick[...], sre_ref[...], preferred_element_type=f32)
    a_im = jnp.dot(pick[...], sim_ref[...], preferred_element_type=f32)
    b_re = bre_ref[...].astype(f32)
    b_im = bim_ref[...].astype(f32)
    length = out_ref.shape[1]
    freq = lax.broadcasted_iota(jnp.int32, (1, TILE), 1) + step * TILE
    scale = jnp.where(freq == 0, 1.0 / length, 2.0 / length).astype(f32)
    total = None
    for product, table in (
        (a_re * b_re - a_im * b_im, tre_ref),
        (a_re * b_im + a_im * b_re, tim_ref),
    ):
        high = product.astype(jnp.bfloat16)
        low = (product - high.astype(f32)).astype(jnp.bfloat16)
        summed = jnp.dot(put[...], high, preferred_element_type=f32)
        summed += jnp.dot(put[...], low, preferred_element_type=f32)
        summed = (summed * scale).astype(jnp.bfloat16)
        part = lax.dot_general(summed, table[...], (((1,), (1,)), ((), ())), preferred_element_type=f32)
        total = part if total is None else total + part

    @pl.when(step == 0)
    def _():
        out_ref[...] = total

    @pl.when(step > 0)
    def _():
        out_ref[...] += total


def predict(a_idx, o_idx, spectra, received, table, rows):
    entries, length = received.shape
    steps = length // 2 // TILE
    whole = lambda j: (0, 0)
    re = lambda j: (0, j)
    im = lambda j: (0, j + steps)
    pair = lambda r: [pl.BlockSpec((r, TILE), re), pl.BlockSpec((r, TILE), im)]
    return pl.pallas_call(
        predict_kernel,
        grid=(steps,),
        in_specs=[
            pl.BlockSpec((entries, 1), whole),
            pl.BlockSpec((1, entries), whole),
            *pair(spectra.shape[0]),
            *pair(entries),
            *pair(length),
        ],
        out_specs=pl.BlockSpec((rows, length), whole),
        out_shape=jax.ShapeDtypeStruct((rows, length), jnp.float32),
        scratch_shapes=[
            pltpu.VMEM((entries, spectra.shape[0]), jnp.bfloat16),
            pltpu.VMEM((rows, entries), jnp.bfloat16),
        ],
        compiler_params=pltpu.CompilerParams(vmem_limit_bytes=VMEM_LIMIT),
    )(a_idx, o_idx, spectra, spectra, received, received, table, table)


def on_device(table, records, source_trace, target_trace, mirror, live_slots):
    shot_dev, rx_local, length = records.shape
    rows = shot_dev * rx_local
    me = lax.axis_index("shot")
    owners, _, slots = source_trace.shape
    send = lax.dynamic_index_in_dim(source_trace, me, 1, False).reshape(-1, 1)
    spec, outgoing = transform(records.reshape(rows, length), send, table)
    spectra = lax.all_gather(spec, "xline", axis=0, tiled=True)
    received = lax.all_to_all(
        outgoing.reshape(owners, slots, length), "shot", split_axis=0, concat_axis=0, tiled=True
    ).reshape(owners * slots, length)
    targets, mirrors = target_trace[0], mirror[0]
    r_local = lax.dynamic_index_in_dim(source_trace, me, 0, False) % rx_local
    live = jnp.arange(slots, dtype=jnp.int32)[None, :] < live_slots[0][:, None]
    a_idx = (mirrors // rx_local * rows + targets * rx_local + mirrors % rx_local).reshape(-1, 1)
    o_idx = jnp.where(live, targets * rx_local + r_local, -1).reshape(1, -1)
    predicted = predict(a_idx, o_idx, spectra, received, table, rows)
    return predicted.reshape(shot_dev, rx_local, length)


def solution(mesh):
    placed = (
        P("shot", "xline", None),
        P(),
        P("shot", None, None),
        P("shot", None, None),
        P("shot", None),
    )

    def run(*args):
        table = jnp.asarray(forward_table(args[0].shape[-1]))
        return jax.shard_map(
            functools.partial(on_device),
            mesh=mesh,
            in_specs=(P(), *placed),
            out_specs=P("shot", "xline", None),
            check_vma=False,
        )(table, *args)

    return run
```

time: 128 us -> 95.8 us (0.75)
  other arithmetic: 73.9 us -> 0.34 us
  waiting for transfers between devices: 0.02 us -> 48.9 us
  Pallas kernels: 0 us -> 19.7 us
  matrix products: 14.3 us -> 0 us
  local copies, waits for them, and re-layouts: 16.8 us -> 4.26 us
    another operation x2 -> x0, other arithmetic: 69.2 us -> none
    all_to_all x1, waiting for transfers between devices: 0.01 us -> 24.7 us  [on_device(): lax.all_to_all(outgoing.reshape(owners, slots, length), 'shot', split_axi...]
    all_gather x1, waiting for transfers between devices: 0.01 us -> 24.2 us  [on_device(): spectra = lax.all_gather(spec, 'xline', axis=0, tiled=True)]
    pallas_call x0 -> x2, Pallas kernels: none -> 19.7 us  [the longest x1 10.9 us: predict(): pl.pallas_call(predict_kernel, grid=(steps,), in_specs=[pl.BlockSpec((ent...]
    dot_general x4 -> x0, matrix products: 14.3 us -> none  [the longest x2 10.1 us: transform(): jnp.dot(block_rows, forward, preferred_element_type=jnp.float32)]
    gather x2 -> x0, local copies, waits for them, and re-layouts: 10.5 us -> none  [the longest x1 7.13 us: on_device(): spec_full.reshape(shot_dev * recv_all, length)]
    convert_element_type x3 -> x0, other arithmetic: 3.18 us -> none  [the longest x1 2.59 us: complex_product(): right = right.astype(jnp.float32)]
    unnamed x21 -> x13, local copies, waits for them, and re-layouts: 5.47 us -> 3.4 us
  transfers between devices with their start and end apart: 2 -> 2, of which waited for: 0 -> 2; matrix products, arithmetic and copies ran while one was open for 40% -> 1% of each run, Pallas kernels for 0% -> 0%
where the time goes in v1:
time: 95.8 us; the launch traced here: 94.5 us
  waiting for transfers between devices  48.9 us (51%)
  Pallas kernels  19.7 us (21%)
  between operations  13.5 us (14%)
  starting transfers between devices  7.77 us (8%)
  local copies, waits for them, and re-layouts  4.26 us (4%)
    all_to_all x1, waiting for transfers between devices, on_device(): lax.all_to_all(outgoing.reshape(owners, slots, length), 'shot', split_axi...  24.7 us
    all_gather x1, waiting for transfers between devices, on_device(): spectra = lax.all_gather(spec, 'xline', axis=0, tiled=True)  24.2 us
    pallas_call x1, Pallas kernels, predict(): pl.pallas_call(predict_kernel, grid=(steps,), in_specs=[pl.BlockSpec((ent...  10.9 us
    pallas_call x1, Pallas kernels, transform(): pl.pallas_call(transform_kernel, grid=(length // TILE,), in_specs=[pl.Blo...  8.77 us
    all_to_all x1, starting transfers between devices, on_device(): lax.all_to_all(outgoing.reshape(owners, slots, length), 'shot', split_axi...  7.77 us
    unnamed x13, local copies, waits for them, and re-layouts  3.4 us
  transfers between devices with their start and end apart: 2, of which 2 were waited for; matrix products, arithmetic and copies ran while one was open for 1% of the time, Pallas kernels for 0%

profile of v1, /device:TPU:2, one launch (start us, length us, event | category | flops | bytes accessed | tf_op | source)
XLA Modules:
  0.0 94.5 jit_solution(1444225800529781328)
XLA Ops:
  6.5 0.0 copy-start
  6.5 0.0 all-gather.2.cloned.1.call-start
  6.5 0.9 %copy-done = s32[32,32,16]{1,2,0:T(8,128)S(1)} copy-done((s32[32,32,16]{1,2,0:T(8,128)S(1)}, s32[32,32,16]{1,2,0:T(8,128)}, u32[]{:S(2)}) %copy-start) | copy-done | bytes 65560
  7.5 0.1 constant_dynamic-slice_fusion
  7.6 0.0 copy-start.2
  7.6 1.0 %copy-done.2 = bf16[2,64,2048]{2,1,0:T(8,128)(2,1)S(1)} copy-done((bf16[2,64,2048]{2,1,0:T(8,128)(2,1)S(1)}, bf16[2,64,2048]{2,1,0:T(8,128)(2,1)}, u32[]{:S(2)}) %copy-start.2) | copy-done | bytes 524312
  8.7 8.8 %shard_map.64 = (bf16[128,2048]{1,0:T(8,128)(2,1)}, bf16[512,2048]{1,0:T(8,128)(2,1)S(1)}) custom-call(s32[512,1]{1,0:T(8,128)S(1)} %bitcast.9, bf16[128,2048]{1,0:T(8,128)(2,1)S(1)} %bitcast.10, bf16[2048,2048]{1,0:T(8,128)(2,1)} %constant.54.clone.table_ref.tre_ref.tim_ref), custom_call_target="tpu_custom_call" | custom-call | tf_op jit(solution)/shard_map/pallas_call | solution.py:40
  17.4 1.3 %copy-done.1 = bf16[512,2048]{1,0:T(8,128)(2,1)} copy-done((bf16[512,2048]{1,0:T(8,128)(2,1)}, bf16[512,2048]{1,0:T(8,128)(2,1)S(1)}, u32[]{:S(2)}) %copy-start.1) | copy-done | bytes 2097176
  18.8 0.0 all-gather.2.cloned.1.call-update
  18.8 7.8 %all-to-all-start = ((bf16[32,16,2048]{2,1,0:T(8,128)(2,1)}), bf16[32,16,2048]{2,1,0:T(8,128)(2,1)S(1)}, u32[]{:S(2)}, u32[]{:S(2)}) async-start(bf16[32,16,2048]{2,1,0:T(8,128)(2,1)} %bitcast.8), calls=%async_computation | async-start | bytes 4194304 | tf_op jit(solution)/shard_map/all_to_all | solution.py:135
  26.6 0.0 copy-done.4
  26.6 0.1 copy.26
  26.7 0.1 mul.41
  26.8 0.2 mul.42
  26.9 0.1 copy.29
  27.0 0.1 squeeze.11
  27.1 0.1 iota_compare_fusion
  27.2 0.1 lt.46
  27.3 0.1 copy.20
  27.3 0.2 squeeze.12
  27.5 0.3 fusion.2.a_idx_ref
  27.8 24.7 %all-to-all-done = bf16[32,16,2048]{2,1,0:T(8,128)(2,1)S(1)} async-done(((bf16[32,16,2048]{2,1,0:T(8,128)(2,1)}), bf16[32,16,2048]{2,1,0:T(8,128)(2,1)S(1)}, u32[]{:S(2)}, u32[]{:S(2)}) %all-to-all-start) | async-done | bytes 2097184 | tf_op jit(solution)/shard_map/all_to_all | solution.py:135
  52.5 24.2 %all-gather.2.cloned.1.call-done.sre_ref.sim_ref = bf16[1024,2048]{1,0:T(8,128)(2,1)} async-done(((bf16[128,2048]{1,0:T(8,128)(2,1)}), bf16[1024,2048]{1,0:T(8,128)(2,1)}) %all-gather.2.cloned.1.call-update) | async-done | bytes 4194320 | tf_op jit(solution)/shard_map/all_gather | solution.py:134
  76.7 10.9 %shard_map.65 = f32[128,2048]{1,0:T(8,128)} custom-call(s32[512,1]{1,0:T(8,128)S(1)} %fusion.2.a_idx_ref, s32[1,512]{1,0:T(1,128)S(1)} %fusion.8.o_idx_ref, bf16[1024,2048]{1,0:T(8,128)(2,1)} %all-gather.2.cloned.1.call-done.sre_ref.sim_ref, bf16[1024,2048]{1,0:T(8,128)(2,1)} %all-gather.2.cloned.1.call-done.sre_ref.sim_ref, bf16[512,2048]{1,0:T(8,128)(2,1)S(1)} %bitcast.6, ...), custom_call_target="tpu_custom_call" | custom-call | tf_op jit(solution)/shard_map/pallas_call | solution.py:107
  (9 shorter events, 0.0 us)
Async XLA Ops:
  6.5 1.0 %copy-start = (s32[32,32,16]{1,2,0:T(8,128)S(1)}, s32[32,32,16]{1,2,0:T(8,128)}, u32[]{:S(2)}) copy-start(s32[32,32,16]{1,2,0:T(8,128)} %param.7) | copy-start | bytes 196612
  6.5 70.2 %all-gather.2.cloned.1.call-start = ((), (), s32[]{:S(2)}) async-start(), calls=%async_computation.1 | async-start | bytes 4718592 | tf_op jit(solution)/shard_map/all_gather | solution.py:134
  7.6 1.0 %copy-start.2 = (bf16[2,64,2048]{2,1,0:T(8,128)(2,1)S(1)}, bf16[2,64,2048]{2,1,0:T(8,128)(2,1)}, u32[]{:S(2)}) copy-start(bf16[2,64,2048]{2,1,0:T(8,128)(2,1)} %param.6) | copy-start | bytes 1572868
  17.4 1.3 %copy-start.1 = (bf16[512,2048]{1,0:T(8,128)(2,1)}, bf16[512,2048]{1,0:T(8,128)(2,1)S(1)}, u32[]{:S(2)}) copy-start(bf16[512,2048]{1,0:T(8,128)(2,1)S(1)} %get-tuple-element.8) | copy-start | bytes 6291460
  18.8 7.8 %copy-start.4 = (s32[1,32,16]{1,2,0:T(8,128)S(1)}, s32[1,32,16]{1,2,0:T(8,128)}, u32[]{:S(2)}) copy-start(s32[1,32,16]{1,2,0:T(8,128)} %param.8) | copy-start | bytes 6148
  18.8 8.3 %copy-start.5 = (s32[1,32]{1,0:T(1,128)S(1)}, s32[1,32]{1,0:T(1,128)}, u32[]{:S(2)}) copy-start(s32[1,32]{1,0:T(1,128)} %param.10) | copy-start | bytes 388
  18.8 8.5 %copy-start.3 = (s32[1,32,16]{1,2,0:T(8,128)S(1)}, s32[1,32,16]{1,2,0:T(8,128)}, u32[]{:S(2)}) copy-start(s32[1,32,16]{1,2,0:T(8,128)} %param.9) | copy-start | bytes 6148
  18.8 33.7 %all-to-all-start = ((bf16[32,16,2048]{2,1,0:T(8,128)(2,1)}), bf16[32,16,2048]{2,1,0:T(8,128)(2,1)S(1)}, u32[]{:S(2)}, u32[]{:S(2)}) async-start(bf16[32,16,2048]{2,1,0:T(8,128)(2,1)} %bitcast.8), calls=%async_computation | async-start | bytes 4194304 | tf_op jit(solution)/shard_map/all_to_all | solution.py:135
Sparse Core Ops, SparseCore 0:
  18.9 57.7 all-gather.1

commit v2 on v0

v2 whole, which is shorter than its diff:
```python
import functools
import math

import jax
import jax.numpy as jnp
import numpy as np
from jax import lax
from jax.experimental import pallas as pl
from jax.experimental.pallas import tpu as pltpu
from jax.sharding import PartitionSpec as P

PARAMS = pltpu.CompilerParams(vmem_limit_bytes=56 * 1024 * 1024)
VMEM = pl.BlockSpec(memory_space=pltpu.VMEM)
ANY = pl.BlockSpec(memory_space=pl.ANY)
TILE = 256
F32 = jnp.float32
BF16 = jnp.bfloat16
CHUNKS = (48, 32)
ROOM = sum(CHUNKS)


def tables(length):
    quarter = length // 4
    t = np.arange(length, dtype=np.int64)[:, None]
    f = np.arange(quarter, dtype=np.int64)[None, :]
    phase = (t * f % length).astype(np.float64) * (2.0 * math.pi / length)
    cos, sin = np.cos(phase), -np.sin(phase)
    turn = t[:, 0] % 4
    sin[:, 0] = np.array([1.0, -1.0, -1.0, 1.0])[turn]
    forward = np.concatenate([cos, sin], axis=1)
    weight = np.full(2 * quarter, 2.0 / length)
    weight[0] = 1.0 / length
    inverse = (forward * weight).T
    return forward.astype(BF16), inverse.astype(BF16)


def dot(left, right):
    return jnp.dot(left, right, preferred_element_type=F32)


def one_hot(left, right):
    return (left == right).astype(F32).astype(BF16)


def iota(shape, axis):
    return lax.broadcasted_iota(jnp.int32, shape, axis)


def tile_at(j, tile=TILE):
    return slice(j * tile, (j + 1) * tile)


def start(source, target, sem):
    copy = pltpu.make_async_copy(source, target, sem)
    copy.start()
    return copy


def open_kernel(xlines, send_ref, want_ref, dest_ref, rec_hbm, table_hbm, *refs):
    out_hbm, *packed_hbm, spec_hbm, full_ref, fast_ref, put_ref = refs[: 5 + len(CHUNKS)]
    rec, table, spec, out, packed, table_sems, out_sems, packed_sems, sems = refs[5 + len(CHUNKS) :]
    count, length = rec.shape
    quarter = length // 4
    first = start(rec_hbm, rec, sems.at[0])
    half = table.shape[0] // 2
    halves = [pl.ds(i * half, half) for i in range(2)]
    coming = [start(table_hbm.at[h], table.at[h], table_sems.at[i]) for i, h in enumerate(halves)]

    owners, slots = send_ref.shape
    entries = owners * slots
    entry, owner = iota((entries, owners), 0), iota((entries, owners), 1)
    spread = ((entry >= owner * slots) & (entry < (owner + 1) * slots)).astype(F32)
    mine = lax.rem(iota((entries, slots), 0), slots) == iota((entries, slots), 1)

    def column(ref):
        wide = jnp.dot(spread, ref[...].astype(F32), precision=lax.Precision.HIGHEST)
        return jnp.sum(jnp.where(mine, wide, 0.0), axis=1, keepdims=True).astype(jnp.int32)

    local = iota((1, count), 1)
    give = one_hot(column(send_ref), local)
    put_ref[...] = (column(dest_ref) == local).astype(F32).T.astype(BF16)
    want = column(want_ref)
    full_ref[...] = want

    named = (want == iota((1, xlines * count), 1)).astype(F32)
    counts = dot(jnp.ones((8, entries), BF16), named.astype(BF16))
    used = jnp.concatenate([counts[:1, tile_at(b, count)] for b in range(xlines)], axis=0) > 0.5
    used = used.astype(F32)
    earlier = (iota((count, count), 0) < iota((count, count), 1)).astype(F32).astype(BF16)
    rank = dot(used.astype(BF16), earlier)
    most = jnp.max(jnp.max(rank + used, axis=1, keepdims=True), axis=0, keepdims=True)
    over = (most > ROOM).astype(F32)
    places = jnp.concatenate([rank[b : b + 1] + float(b * ROOM) for b in range(xlines)], axis=1)
    place = jnp.sum(named * places, axis=1, keepdims=True).astype(jnp.int32)
    fast_ref[...] = jnp.where(want < 0, -1, place)
    pack = ((iota((ROOM, count), 0).astype(F32) == rank[:1]) & (used[:1] > 0.5)).astype(F32).astype(BF16)

    first.wait()
    odd = lax.rem(iota((1, length), 1), 2) == 1
    own = rec[...].astype(F32)
    both = jnp.concatenate([jnp.where(odd, 0.0, own), jnp.where(odd, own, 0.0)], axis=0).astype(BF16)
    for copy in coming:
        copy.wait()
    lane = iota((1, TILE), 1)
    for j in range(quarter // TILE):
        cos = dot(both, table[:, tile_at(j)])
        sin = dot(both, table[:, quarter + j * TILE : quarter + (j + 1) * TILE])
        cos_even, cos_odd, sin_even, sin_odd = cos[:count], cos[count:], sin[:count], sin[count:]
        parts = [cos_even + cos_odd, cos_even - cos_odd, sin_even + sin_odd, sin_odd - sin_even]
        if j == 0:
            parts[1] = jnp.where(lane == 0, sin_even, parts[1])
            parts[2] = jnp.where(lane == 0, 0.0, parts[2])
            parts[3] = jnp.where(lane == 0, sin_odd, parts[3])
        for p, part in enumerate(parts):
            spec[:, p * quarter + j * TILE : p * quarter + (j + 1) * TILE] = part.astype(BF16)
    going = [start(spec, spec_hbm, sems.at[1])]
    for j in range(length // TILE):
        packed[:, tile_at(j)] = dot(pack, spec[:, tile_at(j)]).astype(BF16)
    base = 0
    for i, size in enumerate(CHUNKS):
        going.append(start(packed.at[base : base + size], packed_hbm[i], packed_sems.at[i]))
        base += size
    for j in range(length // TILE):
        rows = dot(give, spec[:, tile_at(j)])
        if j * TILE == 2 * quarter:
            rows = jnp.where(lane == 0, over, rows)
        out[j] = rows.astype(BF16)
        going.append(start(out.at[j], out_hbm.at[:, tile_at(j)], out_sems.at[j]))
    for copy in going:
        copy.wait()


def open_rows(send, want, dest, records, table, xlines):
    count, length = records.shape
    entries = send.size
    steps = length // TILE
    return pl.pallas_call(
        functools.partial(open_kernel, xlines),
        in_specs=[VMEM] * 3 + [ANY] * 2,
        out_specs=[ANY] * (2 + len(CHUNKS)) + [VMEM] * 3,
        out_shape=[
            jax.ShapeDtypeStruct((entries, length), BF16),
            *[jax.ShapeDtypeStruct((size, length), BF16) for size in CHUNKS],
            jax.ShapeDtypeStruct((count, length), BF16),
            jax.ShapeDtypeStruct((entries, 1), jnp.int32),
            jax.ShapeDtypeStruct((entries, 1), jnp.int32),
            jax.ShapeDtypeStruct((count, entries), BF16),
        ],
        scratch_shapes=[
            pltpu.VMEM((count, length), BF16),
            pltpu.VMEM(table.shape, BF16),
            pltpu.VMEM((count, length), BF16),
            pltpu.VMEM((steps, entries, TILE), BF16),
            pltpu.VMEM((ROOM, length), BF16),
            pltpu.SemaphoreType.DMA((2,)),
            pltpu.SemaphoreType.DMA((steps,)),
            pltpu.SemaphoreType.DMA((len(CHUNKS),)),
            pltpu.SemaphoreType.DMA((2,)),
        ],
        compiler_params=PARAMS,
    )(send, want, dest, records, table)


def close_kernel(want_ref, put_ref, inverse_hbm, received_hbm, *refs):
    *chunks, out_ref, rows, received, inverse, total, rows_sems, sems = refs
    length = inverse.shape[1]
    quarter = length // 4
    coming, base = [], 0
    for i, chunk in enumerate(chunks):
        size = chunk.shape[0]
        coming.append(start(chunk, rows.at[base : base + size], rows_sems.at[i]))
        base += size
    other = start(received_hbm, received, sems.at[0])
    take = one_hot(want_ref[...], iota((1, rows.shape[0]), 1))
    for copy in coming:
        copy.wait()
    pieces = [start(inverse_hbm, inverse, sems.at[1])]
    put = put_ref[...]
    count = put.shape[0]
    lane = iota((1, TILE), 1)
    other.wait()
    stacks = []
    for j in range(quarter // TILE):
        sums = []
        for mirror in range(2):
            at = mirror * quarter + j * TILE
            re, im = slice(at, at + TILE), slice(2 * quarter + at, 2 * quarter + at + TILE)
            a_re, a_im = dot(take, rows[:, re]), dot(take, rows[:, im])
            b_re, b_im = received[:, re].astype(F32), received[:, im].astype(F32)
            for product in (a_re * b_re - a_im * b_im, a_re * b_im + a_im * b_re):
                high = product.astype(BF16)
                low = (product - high.astype(F32)).astype(BF16)
                sums.append((dot(put, high) + dot(put, low)).astype(BF16).astype(F32))
        re, im, mirror_re, mirror_im = sums
        even_re, odd_re, even_im, odd_im = re + mirror_re, re - mirror_re, im - mirror_im, im + mirror_im
        if j == 0:
            even_re, odd_re = jnp.where(lane == 0, re, even_re), jnp.where(lane == 0, re, odd_re)
            even_im, odd_im = jnp.where(lane == 0, mirror_re, even_im), jnp.where(lane == 0, mirror_im, odd_im)
        stacks.append(
            [jnp.concatenate(pair, axis=0).astype(BF16) for pair in ((even_re, odd_re), (even_im, odd_im))]
        )
    for copy in pieces:
        copy.wait()
    odd = lax.rem(iota((1, TILE), 1), 2) == 1
    for c in range(length // TILE):
        acc = None
        for j, pair in enumerate(stacks):
            for p, stack in enumerate(pair):
                at = p * quarter + j * TILE
                part = dot(stack, inverse[at : at + TILE, tile_at(c)])
                acc = part if acc is None else acc + part
        out_ref[:, tile_at(c)] = jnp.where(odd, acc[count:], acc[:count])


def close(want, put, inverse, received, chunks):
    entries, length = received.shape
    return pl.pallas_call(
        close_kernel,
        in_specs=[VMEM] * 2 + [ANY] * (2 + len(chunks)),
        out_specs=VMEM,
        out_shape=jax.ShapeDtypeStruct((put.shape[0], length), F32),
        scratch_shapes=[
            pltpu.VMEM((sum(c.shape[0] for c in chunks), length), BF16),
            pltpu.VMEM((entries, length), BF16),
            pltpu.VMEM(inverse.shape, BF16),
            pltpu.VMEM((8, 128), F32),
            pltpu.SemaphoreType.DMA((len(chunks),)),
            pltpu.SemaphoreType.DMA((2,)),
        ],
        compiler_params=PARAMS,
    )(want, put, inverse, received, *chunks)


def ring(parts, xlines):
    up = [(i, (i + 1) % xlines) for i in range(xlines)]
    down = [(i, (i - 1) % xlines) for i in range(xlines)]
    half = xlines // 2
    below, above = list(parts), list(parts)
    chunks = {(0, s): part for s, part in enumerate(parts)}
    for step in range(1, half + 1):
        for s in range(2):
            if step < half or s == 0:
                below[s] = chunks[xlines - step, s] = lax.ppermute(below[s], "xline", up)
            if step < half or s == 1:
                above[s] = chunks[step, s] = lax.ppermute(above[s], "xline", down)
    return [chunks[o, s] for o in range(xlines) for s in range(2)]


def on_device(forward, inverse, records, source_trace, target_trace, mirror, live_slots):
    shot_dev, rx_local, length = records.shape
    count = shot_dev * rx_local
    xlines = lax.axis_size("xline")
    me, line = lax.axis_index("shot"), lax.axis_index("xline")
    owners, _, slots = source_trace.shape

    send = lax.dynamic_index_in_dim(source_trace, me, 1, False)
    r_local = lax.dynamic_index_in_dim(source_trace, me, 0, False) % rx_local
    targets, mirrors = target_trace[0], mirror[0]
    live = jnp.arange(slots, dtype=jnp.int32)[None, :] < live_slots[0][:, None]
    offset = (mirrors // rx_local - line) % xlines
    want = jnp.where(live, offset * count + targets * rx_local + mirrors % rx_local, -1)
    dest = jnp.where(live, targets * rx_local + r_local, -1)
    outgoing, *packed, spectra, full, fast, put = open_rows(
        send, want, dest, records.reshape(count, length), forward, xlines
    )
    received = lax.all_to_all(
        outgoing.reshape(owners, slots, length), "shot", split_axis=0, concat_axis=0, tiled=True
    ).reshape(owners * slots, length)
    chunks = ring(packed, xlines)
    over = jnp.any(received[::slots, length // 2] != 0)

    def whole(received, spectra, full, fast, put, chunks):
        parts = [spectra[: count // 2], spectra[count // 2 :]]
        return close(full, put, inverse, received, ring(parts, xlines))

    def short(received, spectra, full, fast, put, chunks):
        return close(fast, put, inverse, received, chunks)

    predicted = lax.cond(over, whole, short, received, spectra, full, fast, put, chunks)
    return predicted.reshape(shot_dev, rx_local, length)


def solution(mesh):
    placed = (
        P("shot", "xline", None),
        P(),
        P("shot", None, None),
        P("shot", None, None),
        P("shot", None),
    )

    def run(*args):
        forward, inverse = tables(args[0].shape[-1])
        return jax.shard_map(
            on_device,
            mesh=mesh,
            in_specs=(P(), P(), *placed),
            out_specs=P("shot", "xline", None),
            check_vma=False,
        )(jnp.asarray(forward), jnp.asarray(inverse), *args)

    return run
```

time: 128 us -> 70.3 us (0.55)
  other arithmetic: 73.9 us -> 2.06 us
  starting transfers between devices: 7.77 us -> 33.1 us
  Pallas kernels: 0 us -> 15.6 us
  matrix products: 14.3 us -> 0 us
  between operations: 13.6 us -> 0.84 us
  waiting for transfers between devices: 0.02 us -> 12.6 us
  local copies, waits for them, and re-layouts: 16.8 us -> 5.57 us
    another operation x2 -> x0, other arithmetic: 69.2 us -> none
    ppermute x0 -> x14, starting transfers between devices: none -> 25.5 us  [the longest x7 21.4 us: ring(): above[s] = chunks[step, s] = lax.ppermute(above[s], 'xline', down)]
    pallas_call x0 -> x2, Pallas kernels: none -> 15.6 us  [the longest x1 8.2 us: open_rows(): pl.pallas_call(functools.partial(open_kernel, xlines), in_specs=[VMEM] *...]
    dot_general x4 -> x0, matrix products: 14.3 us -> none  [the longest x2 10.1 us: transform(): jnp.dot(block_rows, forward, preferred_element_type=jnp.float32)]
    ppermute x0 -> x14, waiting for transfers between devices: none -> 12.6 us  [the longest x7 8.31 us: ring(): below[s] = chunks[xlines - step, s] = lax.ppermute(below[s], 'xline', up)]
    gather x2 -> x0, local copies, waits for them, and re-layouts: 10.5 us -> none  [the longest x1 7.13 us: on_device(): spec_full.reshape(shot_dev * recv_all, length)]
    convert_element_type x3 -> x0, other arithmetic: 3.18 us -> none  [the longest x1 2.59 us: complex_product(): right = right.astype(jnp.float32)]
    unnamed x21 -> x20, local copies, waits for them, and re-layouts: 5.47 us -> 3.49 us
  transfers between devices with their start and end apart: 2 -> 15, of which waited for: 0 -> 5; matrix products, arithmetic and copies ran while one was open for 40% -> 1% of each run, Pallas kernels for 0% -> 0%
where the time goes in v2:
time: 70.3 us; the launch traced here: 69.8 us
  starting transfers between devices  33.1 us (47%)
  Pallas kernels  15.6 us (22%)
  waiting for transfers between devices  12.6 us (18%)
  local copies, waits for them, and re-layouts  5.57 us (8%)
  other arithmetic  2.06 us (3%)
  between operations  0.84 us (1%)
    ppermute x7, starting transfers between devices, ring(): above[s] = chunks[step, s] = lax.ppermute(above[s], 'xline', down)  21.4 us
    ppermute x7, waiting for transfers between devices, ring(): below[s] = chunks[xlines - step, s] = lax.ppermute(below[s], 'xline', up)  8.31 us
    pallas_call x1, Pallas kernels, open_rows(): pl.pallas_call(functools.partial(open_kernel, xlines), in_specs=[VMEM] *...  8.2 us
    all_to_all x1, starting transfers between devices, on_device(): lax.all_to_all(outgoing.reshape(owners, slots, length), 'shot', split_axi...  7.63 us
    pallas_call x1, Pallas kernels, close(): pl.pallas_call(close_kernel, in_specs=[VMEM] * 2 + [ANY] * (2 + len(chunk...  7.37 us
    ppermute x7, waiting for transfers between devices, ring(): above[s] = chunks[step, s] = lax.ppermute(above[s], 'xline', down)  4.33 us
    ppermute x7, starting transfers between devices, ring(): below[s] = chunks[xlines - step, s] = lax.ppermute(below[s], 'xline', up)  4.12 us
    unnamed x20, local copies, waits for them, and re-layouts  3.49 us
  transfers between devices with their start and end apart: 15, of which 5 were waited for; matrix products, arithmetic and copies ran while one was open for 1% of the time, Pallas kernels for 0%

profile of v2, /device:TPU:2, one launch (start us, length us, event | category | flops | bytes accessed | tf_op | source)
XLA Modules:
  0.0 69.8 jit_solution(15511900599187540487)
XLA Ops:
  0.0 0.9 %copy-done = s32[32,32,16]{1,2,0:T(8,128)S(1)} copy-done((s32[32,32,16]{1,2,0:T(8,128)S(1)}, s32[32,32,16]{1,2,0:T(8,128)}, u32[]{:S(2)}) %copy-start) | copy-done | bytes 65560
  1.2 0.8 %copy.15 = s32[1,32,16]{2,1,0:T(8,128)S(1)} copy(s32[1,32,16]{1,2,0:T(8,128)} %param.11) | data formatting | bytes 4096 | tf_op args[2]
  1.9 0.8 %copy.14 = s32[1,32,16]{2,1,0:T(8,128)S(1)} copy(s32[1,32,16]{1,2,0:T(8,128)} %param.12) | data formatting | bytes 4096 | tf_op args[3]
  2.7 0.9 %copy.19 = s32[32,1,16]{2,0,1:T(8,128)} copy(s32[32,1,16]{1,2,0:T(8,128)S(1)} %constant_dynamic-slice_fusion.1) | data formatting | bytes 4096 | tf_op jit(solution)/shard_map/jit(dynamic_index_in_dim)/squeeze | solution.py:256
  3.6 1.3 %fusion.8 = (s32[32,16]{1,0:T(8,128)}, s32[32,16]{1,0:T(8,128)}) fusion(s32[1,32,16]{2,1,0:T(8,128)S(1)} %copy.16, s32[1,32,16]{2,1,0:T(8,128)S(1)} %copy.15, s32[32]{0:T(128)} %bitcast.41, s32[]{:T(128)S(6)} %axis_index.25, s32[1,32,16]{2,1,0:T(8,128)S(1)} %copy.14), kind=kLoop, calls=%fused_computation.19 | loop fusion | flops 25600 | bytes 10372 | tf_op jit(solution)/shard_map/jit(_where)/select_n | solution.py:262
  4.9 8.2 %shard_map.75 = (bf16[512,2048]{1,0:T(8,128)(2,1)}, bf16[48,2048]{1,0:T(8,128)(2,1)S(1)}, bf16[32,2048]{1,0:T(8,128)(2,1)S(1)}, bf16[128,2048]{1,0:T(8,128)(2,1)...) custom-call(s32[32,16]{1,0:T(8,128)} %bitcast.40, s32[32,16]{1,0:T(8,128)} %get-tuple-element.102.want_ref, ...), custom_call_target="tpu_custom_call" | custom-call | tf_op jit(solution)/shard_map/pallas_call | solution.py:137
  13.1 7.6 %all-to-all-start = ((bf16[32,16,2048]{2,1,0:T(8,128)(2,1)}), bf16[32,16,2048]{2,1,0:T(8,128)(2,1)S(1)}, u32[]{:S(2)}, u32[]{:S(2)}) async-start(bf16[32,16,2048]{2,1,0:T(8,128)(2,1)} %bitcast.36), calls=%async_computation | async-start | bytes 4194304 | tf_op jit(solution)/shard_map/all_to_all | solution.py:266
  20.8 2.0 %collective-permute-start.20 = (bf16[48,2048]{1,0:T(8,128)(2,1)S(1)}, bf16[48,2048]{1,0:T(8,128)(2,1)S(1)}, u32[]{:S(2)}, u32[]{:S(2)}) collective-permute-start(bf16[48,2048]{1,0:T(8,128)(2,1)S(1)} %get-tuple-element.94), channel_id=1, source_target_pairs={{0,1},{1,2},{2,3},{3,4},{4,5},{5,6},{6,7},{7,0},{8,9},{9,10},{10,1... | collective-permute-start | bytes 589832 | tf_op jit(solution)/shard_map/ppermute | solution.py:243
  22.8 4.0 %collective-permute-start.14 = (bf16[48,2048]{1,0:T(8,128)(2,1)S(1)}, bf16[48,2048]{1,0:T(8,128)(2,1)S(1)}, u32[]{:S(2)}, u32[]{:S(2)}) collective-permute-start(bf16[48,2048]{1,0:T(8,128)(2,1)S(1)} %get-tuple-element.94), channel_id=1, source_target_pairs={{0,7},{1,0},{2,1},{3,2},{4,3},{5,4},{6,5},{7,6},{8,15},{9,8},{10,9... | collective-permute-start | bytes 589832 | tf_op jit(solution)/shard_map/ppermute | solution.py:245
  26.8 5.1 %collective-permute-done.20 = bf16[48,2048]{1,0:T(8,128)(2,1)S(1)} collective-permute-done((bf16[48,2048]{1,0:T(8,128)(2,1)S(1)}, bf16[48,2048]{1,0:T(8,128)(2,1)S(1)}, u32[]{:S(2)}, u32[]{:S(2)}) %collective-permute-start.20) | collective-permute-done | bytes 196640 | tf_op jit(solution)/shard_map/ppermute | solution.py:243
  31.9 3.2 %collective-permute-start.15 = (bf16[32,2048]{1,0:T(8,128)(2,1)S(1)}, bf16[32,2048]{1,0:T(8,128)(2,1)S(1)}, u32[]{:S(2)}, u32[]{:S(2)}) collective-permute-start(bf16[32,2048]{1,0:T(8,128)(2,1)S(1)} %get-tuple-element.95), channel_id=1, source_target_pairs={{0,7},{1,0},{2,1},{3,2},{4,3},{5,4},{6,5},{7,6},{8,15},{9,8},{10,9... | collective-permute-start | bytes 393224 | tf_op jit(solution)/shard_map/ppermute | solution.py:245
  35.2 2.5 %collective-permute-done.15 = bf16[32,2048]{1,0:T(8,128)(2,1)S(1)} collective-permute-done((bf16[32,2048]{1,0:T(8,128)(2,1)S(1)}, bf16[32,2048]{1,0:T(8,128)(2,1)S(1)}, u32[]{:S(2)}, u32[]{:S(2)}) %collective-permute-start.15) | collective-permute-done | bytes 131104 | tf_op jit(solution)/shard_map/ppermute | solution.py:245
  37.7 3.7 %collective-permute-start.17 = (bf16[32,2048]{1,0:T(8,128)(2,1)S(1)}, bf16[32,2048]{1,0:T(8,128)(2,1)S(1)}, u32[]{:S(2)}, u32[]{:S(2)}) collective-permute-start(bf16[32,2048]{1,0:T(8,128)(2,1)S(1)} %collective-permute-done.15), channel_id=1, source_target_pairs={{0,7},{1,0},{2,1},{3,2},{4,3},{5,4},{6,5},{7,6},{8,15},{9,8},{10,9... | collective-permute-start | bytes 393224 | tf_op jit(solution)/shard_map/ppermute | solution.py:245
  41.4 1.9 %collective-permute-start.22 = (bf16[48,2048]{1,0:T(8,128)(2,1)S(1)}, bf16[48,2048]{1,0:T(8,128)(2,1)S(1)}, u32[]{:S(2)}, u32[]{:S(2)}) collective-permute-start(bf16[48,2048]{1,0:T(8,128)(2,1)S(1)} %collective-permute-done.21), channel_id=1, source_target_pairs={{0,1},{1,2},{2,3},{3,4},{4,5},{5,6},{6,7},{7,0},{8,9},{9,10},{10,1... | collective-permute-start | bytes 589832 | tf_op jit(solution)/shard_map/ppermute | solution.py:243
  43.5 1.4 %collective-permute-done.17 = bf16[32,2048]{1,0:T(8,128)(2,1)S(1)} collective-permute-done((bf16[32,2048]{1,0:T(8,128)(2,1)S(1)}, bf16[32,2048]{1,0:T(8,128)(2,1)S(1)}, u32[]{:S(2)}, u32[]{:S(2)}) %collective-permute-start.17) | collective-permute-done | bytes 131104 | tf_op jit(solution)/shard_map/ppermute | solution.py:245
  44.9 3.7 %collective-permute-start.19 = (bf16[32,2048]{1,0:T(8,128)(2,1)S(1)}, bf16[32,2048]{1,0:T(8,128)(2,1)}, u32[]{:S(2)}, u32[]{:S(2)}) collective-permute-start(bf16[32,2048]{1,0:T(8,128)(2,1)S(1)} %collective-permute-done.17), channel_id=1, source_target_pairs={{0,7},{1,0},{2,1},{3,2},{4,3},{5,4},{6,5},{7,6},{8,15},{9,8},{10,9... | collective-permute-start | bytes 393224 | tf_op jit(solution)/shard_map/ppermute | solution.py:245
  49.0 3.1 %collective-permute-start.18 = (bf16[48,2048]{1,0:T(8,128)(2,1)S(1)}, bf16[48,2048]{1,0:T(8,128)(2,1)S(1)}, u32[]{:S(2)}, u32[]{:S(2)}) collective-permute-start(bf16[48,2048]{1,0:T(8,128)(2,1)S(1)} %collective-permute-done.16), channel_id=1, source_target_pairs={{0,7},{1,0},{2,1},{3,2},{4,3},{5,4},{6,5},{7,6},{8,15},{9,8},{10,9... | collective-permute-start | bytes 589832 | tf_op jit(solution)/shard_map/ppermute | solution.py:245
  52.2 3.6 %collective-permute-start.24 = (bf16[32,2048]{1,0:T(8,128)(2,1)}, bf16[32,2048]{1,0:T(8,128)(2,1)}, u32[]{:S(2)}, u32[]{:S(2)}) collective-permute-start(bf16[32,2048]{1,0:T(8,128)(2,1)} %collective-permute-done.19), channel_id=1, source_target_pairs={{0,7},{1,0},{2,1},{3,2},{4,3},{5,4},{6,5},{7,6},{8,15},{9,8},{10,9... | collective-permute-start | bytes 393224 | tf_op jit(solution)/shard_map/ppermute | solution.py:245
  55.9 0.7 %compare_reduce_fusion = pred[]{:T(512)} fusion(bf16[32,1]{1,0:T(8,128)(2,1)S(1)} %slice.9), kind=kLoop, calls=%fused_computation.25 | loop fusion | flops 63 | bytes 65 | tf_op jit(solution)/shard_map/reduce_or | solution.py:270
  57.3 3.2 %collective-permute-done.27 = bf16[32,2048]{1,0:T(8,128)(2,1)} collective-permute-done((bf16[32,2048]{1,0:T(8,128)(2,1)}, bf16[32,2048]{1,0:T(8,128)(2,1)}, u32[]{:S(2)}, u32[]{:S(2)}) %collective-permute-start.27) | collective-permute-done | bytes 131104 | tf_op jit(solution)/shard_map/ppermute | solution.py:243
  60.5 8.4 %conditional.1 = (f32[2,64,2048]{2,1,0:T(8,128)S(1)}) conditional(s32[]{:T(128)} %convert_element_type.3, (s32[512,1]{1,0:T(8,128)}, bf16[128,512]{1,0:T(8,128)(2,1)S(1)}, bf16[1024,2048]{1,0:T(8,128)(2,1)}, bf16[512,2048]{1,0:T(8,128)(2,1)S(1)}, bf16[48,2048]{1,0:T(8,128)(2,1)S(1)}, /*index=5*/bf16[32,2048]{1,0:T(8,128)(2,1)}, ...), branch_computations={%region_1.2_spmd, %region_2.3_spmd} | conditional | bytes 32506872 | solution.py:279
  60.5 0.6 copy-done.18
  61.5 7.4 %branch_0_fun.1 = f32[128,2048]{1,0:T(8,128)S(1)} custom-call(s32[512,1]{1,0:T(8,128)} %get-tuple-element.59.want_ref, bf16[128,512]{1,0:T(8,128)(2,1)S(1)} %get-tuple-element.60.put_ref, bf16[1024,2048]{1,0:T(8,128)(2,1)} %get-tuple-element.61.inverse_hbm, bf16[512,2048]{1,0:T(8,128)(2,1)S(1)} %get-tuple-element.62.received_hbm, ...), custom_call_target="tpu_custom_call" | custom-call | tf_op jit(solution)/shard_map/cond/branch_0_fun/pallas_call | solution.py:217
  68.9 1.0 %copy-done.1 = f32[2,64,2048]{2,1,0:T(8,128)} copy-done((f32[2,64,2048]{2,1,0:T(8,128)}, f32[2,64,2048]{2,1,0:T(8,128)S(1)}, u32[]{:S(2)}) %copy-start.1) | copy-done | bytes 1048600
  (46 shorter events, 1.3 us)
Async XLA Ops:
  13.1 35.4 %copy-start.26 = (bf16[32,2048]{1,0:T(8,128)(2,1)}, bf16[32,2048]{1,0:T(8,128)(2,1)S(1)}, u32[]{:S(2)}) copy-start(bf16[32,2048]{1,0:T(8,128)(2,1)S(1)} %get-tuple-element.95) | copy-start | bytes 393220
  13.1 42.7 %all-to-all-start = ((bf16[32,16,2048]{2,1,0:T(8,128)(2,1)}), bf16[32,16,2048]{2,1,0:T(8,128)(2,1)S(1)}, u32[]{:S(2)}, u32[]{:S(2)}) async-start(bf16[32,16,2048]{2,1,0:T(8,128)(2,1)} %bitcast.36), calls=%async_computation | async-start | bytes 4194304 | tf_op jit(solution)/shard_map/all_to_all | solution.py:266
  20.8 11.1 %collective-permute-start.20 = (bf16[48,2048]{1,0:T(8,128)(2,1)S(1)}, bf16[48,2048]{1,0:T(8,128)(2,1)S(1)}, u32[]{:S(2)}, u32[]{:S(2)}) collective-permute-start(bf16[48,2048]{1,0:T(8,128)(2,1)S(1)} %get-tuple-element.94), channel_id=1, source_target_pairs={{0,1},{1,2},{2,3},{3,4},{4,5},{5,6},{6,7},{7,0},{8,9},{9,10},{10,1... | collective-permute-start | bytes 589832 | tf_op jit(solution)/shard_map/ppermute | solution.py:243
  22.8 18.6 %collective-permute-start.14 = (bf16[48,2048]{1,0:T(8,128)(2,1)S(1)}, bf16[48,2048]{1,0:T(8,128)(2,1)S(1)}, u32[]{:S(2)}, u32[]{:S(2)}) collective-permute-start(bf16[48,2048]{1,0:T(8,128)(2,1)S(1)} %get-tuple-element.94), channel_id=1, source_target_pairs={{0,7},{1,0},{2,1},{3,2},{4,3},{5,4},{6,5},{7,6},{8,15},{9,8},{10,9... | collective-permute-start | bytes 589832 | tf_op jit(solution)/shard_map/ppermute | solution.py:245
  31.9 20.3 %copy-start.19 = (bf16[48,2048]{1,0:T(8,128)(2,1)}, bf16[48,2048]{1,0:T(8,128)(2,1)S(1)}, u32[]{:S(2)}) copy-start(bf16[48,2048]{1,0:T(8,128)(2,1)S(1)} %collective-permute-done.20) | copy-start | bytes 589828
  31.9 9.5 %collective-permute-start.21 = (bf16[48,2048]{1,0:T(8,128)(2,1)S(1)}, bf16[48,2048]{1,0:T(8,128)(2,1)S(1)}, u32[]{:S(2)}, u32[]{:S(2)}) collective-permute-start(bf16[48,2048]{1,0:T(8,128)(2,1)S(1)} %collective-permute-done.20), channel_id=1, source_target_pairs={{0,1},{1,2},{2,3},{3,4},{4,5},{5,6},{6,7},{7,0},{8,9},{9,10},{10,1... | collective-permute-start | bytes 589832 | tf_op jit(solution)/shard_map/ppermute | solution.py:243
  31.9 5.8 %collective-permute-start.15 = (bf16[32,2048]{1,0:T(8,128)(2,1)S(1)}, bf16[32,2048]{1,0:T(8,128)(2,1)S(1)}, u32[]{:S(2)}, u32[]{:S(2)}) collective-permute-start(bf16[32,2048]{1,0:T(8,128)(2,1)S(1)} %get-tuple-element.95), channel_id=1, source_target_pairs={{0,7},{1,0},{2,1},{3,2},{4,3},{5,4},{6,5},{7,6},{8,15},{9,8},{10,9... | collective-permute-start | bytes 393224 | tf_op jit(solution)/shard_map/ppermute | solution.py:245
  35.1 8.2 %collective-permute-start.25 = (bf16[32,2048]{1,0:T(8,128)(2,1)S(1)}, bf16[32,2048]{1,0:T(8,128)(2,1)S(1)}, u32[]{:S(2)}, u32[]{:S(2)}) collective-permute-start(bf16[32,2048]{1,0:T(8,128)(2,1)S(1)} %get-tuple-element.95), channel_id=1, source_target_pairs={{0,1},{1,2},{2,3},{3,4},{4,5},{5,6},{6,7},{7,0},{8,9},{9,10},{10,1... | collective-permute-start | bytes 393224 | tf_op jit(solution)/shard_map/ppermute | solution.py:243
  37.7 14.5 %copy-start.27 = (bf16[32,2048]{1,0:T(8,128)(2,1)}, bf16[32,2048]{1,0:T(8,128)(2,1)S(1)}, u32[]{:S(2)}) copy-start(bf16[32,2048]{1,0:T(8,128)(2,1)S(1)} %collective-permute-done.15) | copy-start | bytes 393220
  37.7 7.2 %collective-permute-start.17 = (bf16[32,2048]{1,0:T(8,128)(2,1)S(1)}, bf16[32,2048]{1,0:T(8,128)(2,1)S(1)}, u32[]{:S(2)}, u32[]{:S(2)}) collective-permute-start(bf16[32,2048]{1,0:T(8,128)(2,1)S(1)} %collective-permute-done.15), channel_id=1, source_target_pairs={{0,7},{1,0},{2,1},{3,2},{4,3},{5,4},{6,5},{7,6},{8,15},{9,8},{10,9... | collective-permute-start | bytes 393224 | tf_op jit(solution)/shard_map/ppermute | solution.py:245
  41.3 10.9 %copy-start.20 = (bf16[48,2048]{1,0:T(8,128)(2,1)}, bf16[48,2048]{1,0:T(8,128)(2,1)S(1)}, u32[]{:S(2)}) copy-start(bf16[48,2048]{1,0:T(8,128)(2,1)S(1)} %collective-permute-done.14) | copy-start | bytes 589828
  41.3 7.6 %collective-permute-start.16 = (bf16[48,2048]{1,0:T(8,128)(2,1)S(1)}, bf16[48,2048]{1,0:T(8,128)(2,1)S(1)}, u32[]{:S(2)}, u32[]{:S(2)}) collective-permute-start(bf16[48,2048]{1,0:T(8,128)(2,1)S(1)} %collective-permute-done.14), channel_id=1, source_target_pairs={{0,7},{1,0},{2,1},{3,2},{4,3},{5,4},{6,5},{7,6},{8,15},{9,8},{10,9... | collective-permute-start | bytes 589832 | tf_op jit(solution)/shard_map/ppermute | solution.py:245
  41.4 10.8 %copy-start.21 = (bf16[48,2048]{1,0:T(8,128)(2,1)}, bf16[48,2048]{1,0:T(8,128)(2,1)S(1)}, u32[]{:S(2)}) copy-start(bf16[48,2048]{1,0:T(8,128)(2,1)S(1)} %collective-permute-done.21) | copy-start | bytes 589828
  41.4 10.6 %collective-permute-start.22 = (bf16[48,2048]{1,0:T(8,128)(2,1)S(1)}, bf16[48,2048]{1,0:T(8,128)(2,1)S(1)}, u32[]{:S(2)}, u32[]{:S(2)}) collective-permute-start(bf16[48,2048]{1,0:T(8,128)(2,1)S(1)} %collective-permute-done.21), channel_id=1, source_target_pairs={{0,1},{1,2},{2,3},{3,4},{4,5},{5,6},{6,7},{7,0},{8,9},{9,10},{10,1... | collective-permute-start | bytes 589832 | tf_op jit(solution)/shard_map/ppermute | solution.py:243
  43.4 8.9 %copy-start.28 = (bf16[32,2048]{1,0:T(8,128)(2,1)}, bf16[32,2048]{1,0:T(8,128)(2,1)S(1)}, u32[]{:S(2)}) copy-start(bf16[32,2048]{1,0:T(8,128)(2,1)S(1)} %collective-permute-done.25) | copy-start | bytes 393220
  43.4 8.7 %collective-permute-start.26 = (bf16[32,2048]{1,0:T(8,128)(2,1)S(1)}, bf16[32,2048]{1,0:T(8,128)(2,1)}, u32[]{:S(2)}, u32[]{:S(2)}) collective-permute-start(bf16[32,2048]{1,0:T(8,128)(2,1)S(1)} %collective-permute-done.25), channel_id=1, source_target_pairs={{0,1},{1,2},{2,3},{3,4},{4,5},{5,6},{6,7},{7,0},{8,9},{9,10},{10,1... | collective-permute-start | bytes 393224 | tf_op jit(solution)/shard_map/ppermute | solution.py:243
  44.9 7.4 %copy-start.29 = (bf16[32,2048]{1,0:T(8,128)(2,1)}, bf16[32,2048]{1,0:T(8,128)(2,1)S(1)}, u32[]{:S(2)}) copy-start(bf16[32,2048]{1,0:T(8,128)(2,1)S(1)} %collective-permute-done.17) | copy-start | bytes 393220
  44.9 7.3 %collective-permute-start.19 = (bf16[32,2048]{1,0:T(8,128)(2,1)S(1)}, bf16[32,2048]{1,0:T(8,128)(2,1)}, u32[]{:S(2)}, u32[]{:S(2)}) collective-permute-start(bf16[32,2048]{1,0:T(8,128)(2,1)S(1)} %collective-permute-done.17), channel_id=1, source_target_pairs={{0,7},{1,0},{2,1},{3,2},{4,3},{5,4},{6,5},{7,6},{8,15},{9,8},{10,9... | collective-permute-start | bytes 393224 | tf_op jit(solution)/shard_map/ppermute | solution.py:245
  49.0 11.5 %collective-permute-start.18 = (bf16[48,2048]{1,0:T(8,128)(2,1)S(1)}, bf16[48,2048]{1,0:T(8,128)(2,1)S(1)}, u32[]{:S(2)}, u32[]{:S(2)}) collective-permute-start(bf16[48,2048]{1,0:T(8,128)(2,1)S(1)} %collective-permute-done.16), channel_id=1, source_target_pairs={{0,7},{1,0},{2,1},{3,2},{4,3},{5,4},{6,5},{7,6},{8,15},{9,8},{10,9... | collective-permute-start | bytes 589832 | tf_op jit(solution)/shard_map/ppermute | solution.py:245
  52.1 8.4 %collective-permute-start.23 = (bf16[48,2048]{1,0:T(8,128)(2,1)S(1)}, bf16[48,2048]{1,0:T(8,128)(2,1)S(1)}, u32[]{:S(2)}, u32[]{:S(2)}) collective-permute-start(bf16[48,2048]{1,0:T(8,128)(2,1)S(1)} %collective-permute-done.22), channel_id=1, source_target_pairs={{0,1},{1,2},{2,3},{3,4},{4,5},{5,6},{6,7},{7,0},{8,9},{9,10},{10,1... | collective-permute-start | bytes 589832 | tf_op jit(solution)/shard_map/ppermute | solution.py:243
  52.1 8.4 %collective-permute-start.27 = (bf16[32,2048]{1,0:T(8,128)(2,1)}, bf16[32,2048]{1,0:T(8,128)(2,1)}, u32[]{:S(2)}, u32[]{:S(2)}) collective-permute-start(bf16[32,2048]{1,0:T(8,128)(2,1)} %collective-permute-done.26), channel_id=1, source_target_pairs={{0,1},{1,2},{2,3},{3,4},{4,5},{5,6},{6,7},{7,0},{8,9},{9,10},{10,1... | collective-permute-start | bytes 393224 | tf_op jit(solution)/shard_map/ppermute | solution.py:243
  52.2 8.2 %collective-permute-start.24 = (bf16[32,2048]{1,0:T(8,128)(2,1)}, bf16[32,2048]{1,0:T(8,128)(2,1)}, u32[]{:S(2)}, u32[]{:S(2)}) collective-permute-start(bf16[32,2048]{1,0:T(8,128)(2,1)} %collective-permute-done.19), channel_id=1, source_target_pairs={{0,7},{1,0},{2,1},{3,2},{4,3},{5,4},{6,5},{7,6},{8,15},{9,8},{10,9... | collective-permute-start | bytes 393224 | tf_op jit(solution)/shard_map/ppermute | solution.py:245
  60.5 1.0 %copy-start.25 = (bf16[48,2048]{1,0:T(8,128)(2,1)}, bf16[48,2048]{1,0:T(8,128)(2,1)S(1)}, u32[]{:S(2)}) copy-start(bf16[48,2048]{1,0:T(8,128)(2,1)S(1)} %get-tuple-element.71.refs_8_) | copy-start | bytes 589828 | tf_op jit(solution)/shard_map/cond
  68.9 1.0 %copy-start.1 = (f32[2,64,2048]{2,1,0:T(8,128)}, f32[2,64,2048]{2,1,0:T(8,128)S(1)}, u32[]{:S(2)}) copy-start(f32[2,64,2048]{2,1,0:T(8,128)S(1)} %get-tuple-element.108) | copy-start | bytes 3145732
  (5 other events, 4.0 us)

commit v3 on v2

--- a/solution.py
+++ b/solution.py
@@ -56,7 +56,7 @@
     return copy
 
 
-def open_kernel(xlines, send_ref, want_ref, dest_ref, rec_hbm, table_hbm, *refs):
+def open_kernel(xlines, shots, source_ref, target_ref, mirror_ref, live_ref, rec_hbm, table_hbm, *refs):
     out_hbm, *packed_hbm, spec_hbm, full_ref, fast_ref, put_ref = refs[: 5 + len(CHUNKS)]
     rec, table, spec, out, packed, table_sems, out_sems, packed_sems, sems = refs[5 + len(CHUNKS) :]
     count, length = rec.shape
@@ -66,20 +66,29 @@
     halves = [pl.ds(i * half, half) for i in range(2)]
     coming = [start(table_hbm.at[h], table.at[h], table_sems.at[i]) for i, h in enumerate(halves)]
 
-    owners, slots = send_ref.shape
+    me, line = lax.axis_index("shot"), lax.axis_index("xline")
+    slots, owners = target_ref.shape
     entries = owners * slots
+    spread = (lax.rem(iota((entries, slots), 0), slots) == iota((entries, slots), 1)).astype(F32)
     entry, owner = iota((entries, owners), 0), iota((entries, owners), 1)
-    spread = ((entry >= owner * slots) & (entry < (owner + 1) * slots)).astype(F32)
-    mine = lax.rem(iota((entries, slots), 0), slots) == iota((entries, slots), 1)
-
-    def column(ref):
-        wide = jnp.dot(spread, ref[...].astype(F32), precision=lax.Precision.HIGHEST)
+    mine = (entry >= owner * slots) & (entry < (owner + 1) * slots)
+
+    def column(values):
+        wide = jnp.dot(spread, values.astype(F32), precision=lax.Precision.HIGHEST)
         return jnp.sum(jnp.where(mine, wide, 0.0), axis=1, keepdims=True).astype(jnp.int32)
 
     local = iota((1, count), 1)
-    give = one_hot(column(send_ref), local)
-    put_ref[...] = (column(dest_ref) == local).astype(F32).T.astype(BF16)
-    want = column(want_ref)
+    rx_local = count // shots
+    live = iota((slots, owners), 0) < live_ref[...]
+    target, mirrored = target_ref[...], mirror_ref[...]
+    used_here = source_ref[pl.ds(pl.multiple_of(me * slots, slots), slots), :]
+    dest = jnp.where(live, target * rx_local + lax.rem(used_here, rx_local), -1)
+    offset = lax.rem(lax.div(mirrored, rx_local) + xlines - line, xlines)
+    want = jnp.where(live, offset * count + target * rx_local + lax.rem(mirrored, rx_local), -1)
+    send = jnp.sum(jnp.where(owner == me, source_ref[...], 0), axis=1, keepdims=True)
+    give = one_hot(send, local)
+    put_ref[...] = (column(dest) == local).astype(F32).T.astype(BF16)
+    want = column(want)
     full_ref[...] = want
 
     named = (want == iota((1, xlines * count), 1)).astype(F32)
@@ -130,13 +139,13 @@
         copy.wait()
 
 
-def open_rows(send, want, dest, records, table, xlines):
+def open_rows(source, target, mirror, live, records, table, xlines, shots):
     count, length = records.shape
-    entries = send.size
+    entries = source.shape[0]
     steps = length // TILE
     return pl.pallas_call(
-        functools.partial(open_kernel, xlines),
-        in_specs=[VMEM] * 3 + [ANY] * 2,
+        functools.partial(open_kernel, xlines, shots),
+        in_specs=[VMEM] * 4 + [ANY] * 2,
         out_specs=[ANY] * (2 + len(CHUNKS)) + [VMEM] * 3,
         out_shape=[
             jax.ShapeDtypeStruct((entries, length), BF16),
@@ -158,11 +167,11 @@
             pltpu.SemaphoreType.DMA((2,)),
         ],
         compiler_params=PARAMS,
-    )(send, want, dest, records, table)
+    )(source, target, mirror, live, records, table)
 
 
 def close_kernel(want_ref, put_ref, inverse_hbm, received_hbm, *refs):
-    *chunks, out_ref, rows, received, inverse, total, rows_sems, sems = refs
+    *chunks, out_ref, rows, received, inverse, rows_sems, sems = refs
     length = inverse.shape[1]
     quarter = length // 4
     coming, base = [], 0
@@ -199,8 +208,7 @@
         stacks.append(
             [jnp.concatenate(pair, axis=0).astype(BF16) for pair in ((even_re, odd_re), (even_im, odd_im))]
         )
-    for copy in pieces:
-        copy.wait()
+    pieces[0].wait()
     odd = lax.rem(iota((1, TILE), 1), 2) == 1
     for c in range(length // TILE):
         acc = None
@@ -223,7 +231,6 @@
             pltpu.VMEM((sum(c.shape[0] for c in chunks), length), BF16),
             pltpu.VMEM((entries, length), BF16),
             pltpu.VMEM(inverse.shape, BF16),
-            pltpu.VMEM((8, 128), F32),
             pltpu.SemaphoreType.DMA((len(chunks),)),
             pltpu.SemaphoreType.DMA((2,)),
         ],
@@ -250,18 +257,17 @@
     shot_dev, rx_local, length = records.shape
     count = shot_dev * rx_local
     xlines = lax.axis_size("xline")
-    me, line = lax.axis_index("shot"), lax.axis_index("xline")
     owners, _, slots = source_trace.shape
-
-    send = lax.dynamic_index_in_dim(source_trace, me, 1, False)
-    r_local = lax.dynamic_index_in_dim(source_trace, me, 0, False) % rx_local
-    targets, mirrors = target_trace[0], mirror[0]
-    live = jnp.arange(slots, dtype=jnp.int32)[None, :] < live_slots[0][:, None]
-    offset = (mirrors // rx_local - line) % xlines
-    want = jnp.where(live, offset * count + targets * rx_local + mirrors % rx_local, -1)
-    dest = jnp.where(live, targets * rx_local + r_local, -1)
+    source = source_trace.transpose(0, 2, 1).reshape(owners * slots, owners)
     outgoing, *packed, spectra, full, fast, put = open_rows(
-        send, want, dest, records.reshape(count, length), forward, xlines
+        source,
+        target_trace[0].T,
+        mirror[0].T,
+        live_slots,
+        records.reshape(count, length),
+        forward,
+        xlines,
+        shot_dev,
     )
     received = lax.all_to_all(
         outgoing.reshape(owners, slots, length), "shot", split_axis=0, concat_axis=0, tiled=True

time: 70.3 us -> 66 us (0.939)
  local copies, waits for them, and re-layouts: 5.57 us -> 2.01 us
  other arithmetic: 2.06 us -> 0.64 us
  Pallas kernels: 15.6 us -> 16.4 us
    unnamed x20 -> x16, local copies, waits for them, and re-layouts: 3.49 us -> 0.99 us
    select_n x1 -> x0, other arithmetic: 1.34 us -> none  [on_device(): dest = jnp.where(live, targets * rx_local + r_local, -1)]
    squeeze x1 -> x0, local copies, waits for them, and re-layouts: 0.85 us -> none  [on_device(): send = lax.dynamic_index_in_dim(source_trace, me, 1, False)]
    pallas_call x1, Pallas kernels: 8.2 us -> 8.99 us  [open_rows(): pl.pallas_call(functools.partial(open_kernel, xlines, shots), in_specs=[V...]
where the time goes in v3:
time: 66 us; the launch traced here: 65.7 us
  starting transfers between devices  33.1 us (50%)
  Pallas kernels  16.4 us (25%)
  waiting for transfers between devices  12.8 us (19%)
  local copies, waits for them, and re-layouts  2.01 us (3%)
  between operations  0.69 us (1%)
    ppermute x7, starting transfers between devices, ring(): above[s] = chunks[step, s] = lax.ppermute(above[s], 'xline', down)  21.4 us
    pallas_call x1, Pallas kernels, open_rows(): pl.pallas_call(functools.partial(open_kernel, xlines, shots), in_specs=[V...  8.99 us
    ppermute x7, waiting for transfers between devices, ring(): below[s] = chunks[xlines - step, s] = lax.ppermute(below[s], 'xline', up)  8.52 us
    all_to_all x1, starting transfers between devices, on_device(): lax.all_to_all(outgoing.reshape(owners, slots, length), 'shot', split_axi...  7.63 us
    pallas_call x1, Pallas kernels, close(): pl.pallas_call(close_kernel, in_specs=[VMEM] * 2 + [ANY] * (2 + len(chunk...  7.37 us
    ppermute x7, waiting for transfers between devices, ring(): above[s] = chunks[step, s] = lax.ppermute(above[s], 'xline', down)  4.33 us
    ppermute x7, starting transfers between devices, ring(): below[s] = chunks[xlines - step, s] = lax.ppermute(below[s], 'xline', up)  4.12 us
  transfers between devices with their start and end apart: 15, of which 5 were waited for; matrix products, arithmetic and copies ran while one was open for 1% of the time, Pallas kernels for 0%

profile of v3, /device:TPU:2, one launch (start us, length us, event | category | flops | bytes accessed | tf_op | source)
XLA Modules:
  0.0 65.7 jit_solution(2392019507161281788)
XLA Ops:
  0.0 9.0 %shard_map.75 = (bf16[512,2048]{1,0:T(8,128)(2,1)}, bf16[48,2048]{1,0:T(8,128)(2,1)S(1)}, bf16[32,2048]{1,0:T(8,128)(2,1)S(1)}, bf16[128,2048]{1,0:T(8,128)(2,1)...) custom-call(s32[512,32]{1,0:T(8,128)} %bitcast.21, s32[16,32]{1,0:T(8,128)} %bitcast.22, ...), custom_call_target="tpu_custom_call" | custom-call | tf_op jit(solution)/shard_map/pallas_call | solution.py:146
  9.0 7.6 %all-to-all-start = ((bf16[32,16,2048]{2,1,0:T(8,128)(2,1)}), bf16[32,16,2048]{2,1,0:T(8,128)(2,1)S(1)}, u32[]{:S(2)}, u32[]{:S(2)}) async-start(bf16[32,16,2048]{2,1,0:T(8,128)(2,1)} %bitcast.17), calls=%async_computation | async-start | bytes 4194304 | tf_op jit(solution)/shard_map/all_to_all | solution.py:272
  16.6 2.0 %collective-permute-start.20 = (bf16[48,2048]{1,0:T(8,128)(2,1)S(1)}, bf16[48,2048]{1,0:T(8,128)(2,1)S(1)}, u32[]{:S(2)}, u32[]{:S(2)}) collective-permute-start(bf16[48,2048]{1,0:T(8,128)(2,1)S(1)} %get-tuple-element.94), channel_id=1, source_target_pairs={{0,1},{1,2},{2,3},{3,4},{4,5},{5,6},{6,7},{7,0},{8,9},{9,10},{10,1... | collective-permute-start | bytes 589832 | tf_op jit(solution)/shard_map/ppermute | solution.py:250
  18.6 4.0 %collective-permute-start.14 = (bf16[48,2048]{1,0:T(8,128)(2,1)S(1)}, bf16[48,2048]{1,0:T(8,128)(2,1)S(1)}, u32[]{:S(2)}, u32[]{:S(2)}) collective-permute-start(bf16[48,2048]{1,0:T(8,128)(2,1)S(1)} %get-tuple-element.94), channel_id=1, source_target_pairs={{0,7},{1,0},{2,1},{3,2},{4,3},{5,4},{6,5},{7,6},{8,15},{9,8},{10,9... | collective-permute-start | bytes 589832 | tf_op jit(solution)/shard_map/ppermute | solution.py:252
  22.7 5.1 %collective-permute-done.20 = bf16[48,2048]{1,0:T(8,128)(2,1)S(1)} collective-permute-done((bf16[48,2048]{1,0:T(8,128)(2,1)S(1)}, bf16[48,2048]{1,0:T(8,128)(2,1)S(1)}, u32[]{:S(2)}, u32[]{:S(2)}) %collective-permute-start.20) | collective-permute-done | bytes 196640 | tf_op jit(solution)/shard_map/ppermute | solution.py:250
  27.8 3.2 %collective-permute-start.15 = (bf16[32,2048]{1,0:T(8,128)(2,1)S(1)}, bf16[32,2048]{1,0:T(8,128)(2,1)S(1)}, u32[]{:S(2)}, u32[]{:S(2)}) collective-permute-start(bf16[32,2048]{1,0:T(8,128)(2,1)S(1)} %get-tuple-element.95), channel_id=1, source_target_pairs={{0,7},{1,0},{2,1},{3,2},{4,3},{5,4},{6,5},{7,6},{8,15},{9,8},{10,9... | collective-permute-start | bytes 393224 | tf_op jit(solution)/shard_map/ppermute | solution.py:252
  31.0 2.5 %collective-permute-done.15 = bf16[32,2048]{1,0:T(8,128)(2,1)S(1)} collective-permute-done((bf16[32,2048]{1,0:T(8,128)(2,1)S(1)}, bf16[32,2048]{1,0:T(8,128)(2,1)S(1)}, u32[]{:S(2)}, u32[]{:S(2)}) %collective-permute-start.15) | collective-permute-done | bytes 131104 | tf_op jit(solution)/shard_map/ppermute | solution.py:252
  33.6 3.7 %collective-permute-start.17 = (bf16[32,2048]{1,0:T(8,128)(2,1)S(1)}, bf16[32,2048]{1,0:T(8,128)(2,1)S(1)}, u32[]{:S(2)}, u32[]{:S(2)}) collective-permute-start(bf16[32,2048]{1,0:T(8,128)(2,1)S(1)} %collective-permute-done.15), channel_id=1, source_target_pairs={{0,7},{1,0},{2,1},{3,2},{4,3},{5,4},{6,5},{7,6},{8,15},{9,8},{10,9... | collective-permute-start | bytes 393224 | tf_op jit(solution)/shard_map/ppermute | solution.py:252
  37.2 0.1 collective-permute-start.16
  37.3 1.9 %collective-permute-start.22 = (bf16[48,2048]{1,0:T(8,128)(2,1)S(1)}, bf16[48,2048]{1,0:T(8,128)(2,1)S(1)}, u32[]{:S(2)}, u32[]{:S(2)}) collective-permute-start(bf16[48,2048]{1,0:T(8,128)(2,1)S(1)} %collective-permute-done.21), channel_id=1, source_target_pairs={{0,1},{1,2},{2,3},{3,4},{4,5},{5,6},{6,7},{7,0},{8,9},{9,10},{10,1... | collective-permute-start | bytes 589832 | tf_op jit(solution)/shard_map/ppermute | solution.py:250
  39.3 0.1 collective-permute-start.26
  39.4 1.4 %collective-permute-done.17 = bf16[32,2048]{1,0:T(8,128)(2,1)S(1)} collective-permute-done((bf16[32,2048]{1,0:T(8,128)(2,1)S(1)}, bf16[32,2048]{1,0:T(8,128)(2,1)S(1)}, u32[]{:S(2)}, u32[]{:S(2)}) %collective-permute-start.17) | collective-permute-done | bytes 131104 | tf_op jit(solution)/shard_map/ppermute | solution.py:252
  40.8 3.7 %collective-permute-start.19 = (bf16[32,2048]{1,0:T(8,128)(2,1)S(1)}, bf16[32,2048]{1,0:T(8,128)(2,1)}, u32[]{:S(2)}, u32[]{:S(2)}) collective-permute-start(bf16[32,2048]{1,0:T(8,128)(2,1)S(1)} %collective-permute-done.17), channel_id=1, source_target_pairs={{0,7},{1,0},{2,1},{3,2},{4,3},{5,4},{6,5},{7,6},{8,15},{9,8},{10,9... | collective-permute-start | bytes 393224 | tf_op jit(solution)/shard_map/ppermute | solution.py:252
  44.4 0.4 collective-permute-done.16
  44.9 3.1 %collective-permute-start.18 = (bf16[48,2048]{1,0:T(8,128)(2,1)S(1)}, bf16[48,2048]{1,0:T(8,128)(2,1)S(1)}, u32[]{:S(2)}, u32[]{:S(2)}) collective-permute-start(bf16[48,2048]{1,0:T(8,128)(2,1)S(1)} %collective-permute-done.16), channel_id=1, source_target_pairs={{0,7},{1,0},{2,1},{3,2},{4,3},{5,4},{6,5},{7,6},{8,15},{9,8},{10,9... | collective-permute-start | bytes 589832 | tf_op jit(solution)/shard_map/ppermute | solution.py:252
  48.0 0.1 collective-permute-start.27
  48.1 3.6 %collective-permute-start.24 = (bf16[32,2048]{1,0:T(8,128)(2,1)}, bf16[32,2048]{1,0:T(8,128)(2,1)}, u32[]{:S(2)}, u32[]{:S(2)}) collective-permute-start(bf16[32,2048]{1,0:T(8,128)(2,1)} %collective-permute-done.19), channel_id=1, source_target_pairs={{0,7},{1,0},{2,1},{3,2},{4,3},{5,4},{6,5},{7,6},{8,15},{9,8},{10,9... | collective-permute-start | bytes 393224 | tf_op jit(solution)/shard_map/ppermute | solution.py:252
  51.8 0.6 compare_reduce_fusion
  53.0 3.4 %collective-permute-done.27 = bf16[32,2048]{1,0:T(8,128)(2,1)} collective-permute-done((bf16[32,2048]{1,0:T(8,128)(2,1)}, bf16[32,2048]{1,0:T(8,128)(2,1)}, u32[]{:S(2)}, u32[]{:S(2)}) %collective-permute-start.27) | collective-permute-done | bytes 131104 | tf_op jit(solution)/shard_map/ppermute | solution.py:250
  56.4 8.4 %conditional.1 = (f32[2,64,2048]{2,1,0:T(8,128)S(1)}) conditional(s32[]{:T(128)} %convert_element_type.3, (s32[512,1]{1,0:T(8,128)}, bf16[128,512]{1,0:T(8,128)(2,1)S(1)}, bf16[1024,2048]{1,0:T(8,128)(2,1)}, bf16[512,2048]{1,0:T(8,128)(2,1)S(1)}, bf16[48,2048]{1,0:T(8,128)(2,1)S(1)}, /*index=5*/bf16[32,2048]{1,0:T(8,128)(2,1)}, ...), branch_computations={%region_1.0_spmd, %region_2.0_spmd} | conditional | bytes 32506872 | solution.py:285
  56.4 0.6 copy-done.17
  57.2 0.1 copy-done.23
  57.4 7.4 %branch_0_fun.1 = f32[128,2048]{1,0:T(8,128)S(1)} custom-call(s32[512,1]{1,0:T(8,128)} %get-tuple-element.59.want_ref, bf16[128,512]{1,0:T(8,128)(2,1)S(1)} %get-tuple-element.60.put_ref, bf16[1024,2048]{1,0:T(8,128)(2,1)} %get-tuple-element.61.inverse_hbm, bf16[512,2048]{1,0:T(8,128)(2,1)S(1)} %get-tuple-element.62.received_hbm, ...), custom_call_target="tpu_custom_call" | custom-call | tf_op jit(solution)/shard_map/cond/branch_0_fun/pallas_call | solution.py:225
  64.8 1.0 %copy-done = f32[2,64,2048]{2,1,0:T(8,128)} copy-done((f32[2,64,2048]{2,1,0:T(8,128)}, f32[2,64,2048]{2,1,0:T(8,128)S(1)}, u32[]{:S(2)}) %copy-start) | copy-done | bytes 1048600
  (37 shorter events, 0.4 us)
Async XLA Ops:
  9.0 35.4 %copy-start.25 = (bf16[32,2048]{1,0:T(8,128)(2,1)}, bf16[32,2048]{1,0:T(8,128)(2,1)S(1)}, u32[]{:S(2)}) copy-start(bf16[32,2048]{1,0:T(8,128)(2,1)S(1)} %get-tuple-element.95) | copy-start | bytes 393220
  9.0 42.7 %all-to-all-start = ((bf16[32,16,2048]{2,1,0:T(8,128)(2,1)}), bf16[32,16,2048]{2,1,0:T(8,128)(2,1)S(1)}, u32[]{:S(2)}, u32[]{:S(2)}) async-start(bf16[32,16,2048]{2,1,0:T(8,128)(2,1)} %bitcast.17), calls=%async_computation | async-start | bytes 4194304 | tf_op jit(solution)/shard_map/all_to_all | solution.py:272
  16.6 11.1 %collective-permute-start.20 = (bf16[48,2048]{1,0:T(8,128)(2,1)S(1)}, bf16[48,2048]{1,0:T(8,128)(2,1)S(1)}, u32[]{:S(2)}, u32[]{:S(2)}) collective-permute-start(bf16[48,2048]{1,0:T(8,128)(2,1)S(1)} %get-tuple-element.94), channel_id=1, source_target_pairs={{0,1},{1,2},{2,3},{3,4},{4,5},{5,6},{6,7},{7,0},{8,9},{9,10},{10,1... | collective-permute-start | bytes 589832 | tf_op jit(solution)/shard_map/ppermute | solution.py:250
  18.6 18.6 %collective-permute-start.14 = (bf16[48,2048]{1,0:T(8,128)(2,1)S(1)}, bf16[48,2048]{1,0:T(8,128)(2,1)S(1)}, u32[]{:S(2)}, u32[]{:S(2)}) collective-permute-start(bf16[48,2048]{1,0:T(8,128)(2,1)S(1)} %get-tuple-element.94), channel_id=1, source_target_pairs={{0,7},{1,0},{2,1},{3,2},{4,3},{5,4},{6,5},{7,6},{8,15},{9,8},{10,9... | collective-permute-start | bytes 589832 | tf_op jit(solution)/shard_map/ppermute | solution.py:252
  27.8 20.3 %copy-start.18 = (bf16[48,2048]{1,0:T(8,128)(2,1)}, bf16[48,2048]{1,0:T(8,128)(2,1)S(1)}, u32[]{:S(2)}) copy-start(bf16[48,2048]{1,0:T(8,128)(2,1)S(1)} %collective-permute-done.20) | copy-start | bytes 589828
  27.8 9.5 %collective-permute-start.21 = (bf16[48,2048]{1,0:T(8,128)(2,1)S(1)}, bf16[48,2048]{1,0:T(8,128)(2,1)S(1)}, u32[]{:S(2)}, u32[]{:S(2)}) collective-permute-start(bf16[48,2048]{1,0:T(8,128)(2,1)S(1)} %collective-permute-done.20), channel_id=1, source_target_pairs={{0,1},{1,2},{2,3},{3,4},{4,5},{5,6},{6,7},{7,0},{8,9},{9,10},{10,1... | collective-permute-start | bytes 589832 | tf_op jit(solution)/shard_map/ppermute | solution.py:250
  27.8 5.8 %collective-permute-start.15 = (bf16[32,2048]{1,0:T(8,128)(2,1)S(1)}, bf16[32,2048]{1,0:T(8,128)(2,1)S(1)}, u32[]{:S(2)}, u32[]{:S(2)}) collective-permute-start(bf16[32,2048]{1,0:T(8,128)(2,1)S(1)} %get-tuple-element.95), channel_id=1, source_target_pairs={{0,7},{1,0},{2,1},{3,2},{4,3},{5,4},{6,5},{7,6},{8,15},{9,8},{10,9... | collective-permute-start | bytes 393224 | tf_op jit(solution)/shard_map/ppermute | solution.py:252
  31.0 8.2 %collective-permute-start.25 = (bf16[32,2048]{1,0:T(8,128)(2,1)S(1)}, bf16[32,2048]{1,0:T(8,128)(2,1)S(1)}, u32[]{:S(2)}, u32[]{:S(2)}) collective-permute-start(bf16[32,2048]{1,0:T(8,128)(2,1)S(1)} %get-tuple-element.95), channel_id=1, source_target_pairs={{0,1},{1,2},{2,3},{3,4},{4,5},{5,6},{6,7},{7,0},{8,9},{9,10},{10,1... | collective-permute-start | bytes 393224 | tf_op jit(solution)/shard_map/ppermute | solution.py:250
  33.6 14.5 %copy-start.26 = (bf16[32,2048]{1,0:T(8,128)(2,1)}, bf16[32,2048]{1,0:T(8,128)(2,1)S(1)}, u32[]{:S(2)}) copy-start(bf16[32,2048]{1,0:T(8,128)(2,1)S(1)} %collective-permute-done.15) | copy-start | bytes 393220
  33.6 7.2 %collective-permute-start.17 = (bf16[32,2048]{1,0:T(8,128)(2,1)S(1)}, bf16[32,2048]{1,0:T(8,128)(2,1)S(1)}, u32[]{:S(2)}, u32[]{:S(2)}) collective-permute-start(bf16[32,2048]{1,0:T(8,128)(2,1)S(1)} %collective-permute-done.15), channel_id=1, source_target_pairs={{0,7},{1,0},{2,1},{3,2},{4,3},{5,4},{6,5},{7,6},{8,15},{9,8},{10,9... | collective-permute-start | bytes 393224 | tf_op jit(solution)/shard_map/ppermute | solution.py:252
  37.2 10.9 %copy-start.19 = (bf16[48,2048]{1,0:T(8,128)(2,1)}, bf16[48,2048]{1,0:T(8,128)(2,1)S(1)}, u32[]{:S(2)}) copy-start(bf16[48,2048]{1,0:T(8,128)(2,1)S(1)} %collective-permute-done.14) | copy-start | bytes 589828
  37.2 7.6 %collective-permute-start.16 = (bf16[48,2048]{1,0:T(8,128)(2,1)S(1)}, bf16[48,2048]{1,0:T(8,128)(2,1)S(1)}, u32[]{:S(2)}, u32[]{:S(2)}) collective-permute-start(bf16[48,2048]{1,0:T(8,128)(2,1)S(1)} %collective-permute-done.14), channel_id=1, source_target_pairs={{0,7},{1,0},{2,1},{3,2},{4,3},{5,4},{6,5},{7,6},{8,15},{9,8},{10,9... | collective-permute-start | bytes 589832 | tf_op jit(solution)/shard_map/ppermute | solution.py:252
  37.3 10.8 %copy-start.20 = (bf16[48,2048]{1,0:T(8,128)(2,1)}, bf16[48,2048]{1,0:T(8,128)(2,1)S(1)}, u32[]{:S(2)}) copy-start(bf16[48,2048]{1,0:T(8,128)(2,1)S(1)} %collective-permute-done.21) | copy-start | bytes 589828
  37.3 10.6 %collective-permute-start.22 = (bf16[48,2048]{1,0:T(8,128)(2,1)S(1)}, bf16[48,2048]{1,0:T(8,128)(2,1)S(1)}, u32[]{:S(2)}, u32[]{:S(2)}) collective-permute-start(bf16[48,2048]{1,0:T(8,128)(2,1)S(1)} %collective-permute-done.21), channel_id=1, source_target_pairs={{0,1},{1,2},{2,3},{3,4},{4,5},{5,6},{6,7},{7,0},{8,9},{9,10},{10,1... | collective-permute-start | bytes 589832 | tf_op jit(solution)/shard_map/ppermute | solution.py:250
  39.3 8.9 %copy-start.27 = (bf16[32,2048]{1,0:T(8,128)(2,1)}, bf16[32,2048]{1,0:T(8,128)(2,1)S(1)}, u32[]{:S(2)}) copy-start(bf16[32,2048]{1,0:T(8,128)(2,1)S(1)} %collective-permute-done.25) | copy-start | bytes 393220
  39.3 8.7 %collective-permute-start.26 = (bf16[32,2048]{1,0:T(8,128)(2,1)S(1)}, bf16[32,2048]{1,0:T(8,128)(2,1)}, u32[]{:S(2)}, u32[]{:S(2)}) collective-permute-start(bf16[32,2048]{1,0:T(8,128)(2,1)S(1)} %collective-permute-done.25), channel_id=1, source_target_pairs={{0,1},{1,2},{2,3},{3,4},{4,5},{5,6},{6,7},{7,0},{8,9},{9,10},{10,1... | collective-permute-start | bytes 393224 | tf_op jit(solution)/shard_map/ppermute | solution.py:250
  40.7 7.4 %copy-start.28 = (bf16[32,2048]{1,0:T(8,128)(2,1)}, bf16[32,2048]{1,0:T(8,128)(2,1)S(1)}, u32[]{:S(2)}) copy-start(bf16[32,2048]{1,0:T(8,128)(2,1)S(1)} %collective-permute-done.17) | copy-start | bytes 393220
  40.8 7.3 %collective-permute-start.19 = (bf16[32,2048]{1,0:T(8,128)(2,1)S(1)}, bf16[32,2048]{1,0:T(8,128)(2,1)}, u32[]{:S(2)}, u32[]{:S(2)}) collective-permute-start(bf16[32,2048]{1,0:T(8,128)(2,1)S(1)} %collective-permute-done.17), channel_id=1, source_target_pairs={{0,7},{1,0},{2,1},{3,2},{4,3},{5,4},{6,5},{7,6},{8,15},{9,8},{10,9... | collective-permute-start | bytes 393224 | tf_op jit(solution)/shard_map/ppermute | solution.py:252
  44.9 11.5 %collective-permute-start.18 = (bf16[48,2048]{1,0:T(8,128)(2,1)S(1)}, bf16[48,2048]{1,0:T(8,128)(2,1)S(1)}, u32[]{:S(2)}, u32[]{:S(2)}) collective-permute-start(bf16[48,2048]{1,0:T(8,128)(2,1)S(1)} %collective-permute-done.16), channel_id=1, source_target_pairs={{0,7},{1,0},{2,1},{3,2},{4,3},{5,4},{6,5},{7,6},{8,15},{9,8},{10,9... | collective-permute-start | bytes 589832 | tf_op jit(solution)/shard_map/ppermute | solution.py:252
  48.0 8.4 %collective-permute-start.23 = (bf16[48,2048]{1,0:T(8,128)(2,1)S(1)}, bf16[48,2048]{1,0:T(8,128)(2,1)S(1)}, u32[]{:S(2)}, u32[]{:S(2)}) collective-permute-start(bf16[48,2048]{1,0:T(8,128)(2,1)S(1)} %collective-permute-done.22), channel_id=1, source_target_pairs={{0,1},{1,2},{2,3},{3,4},{4,5},{5,6},{6,7},{7,0},{8,9},{9,10},{10,1... | collective-permute-start | bytes 589832 | tf_op jit(solution)/shard_map/ppermute | solution.py:250
  48.0 8.4 %collective-permute-start.27 = (bf16[32,2048]{1,0:T(8,128)(2,1)}, bf16[32,2048]{1,0:T(8,128)(2,1)}, u32[]{:S(2)}, u32[]{:S(2)}) collective-permute-start(bf16[32,2048]{1,0:T(8,128)(2,1)} %collective-permute-done.26), channel_id=1, source_target_pairs={{0,1},{1,2},{2,3},{3,4},{4,5},{5,6},{6,7},{7,0},{8,9},{9,10},{10,1... | collective-permute-start | bytes 393224 | tf_op jit(solution)/shard_map/ppermute | solution.py:250
  48.1 8.2 %collective-permute-start.24 = (bf16[32,2048]{1,0:T(8,128)(2,1)}, bf16[32,2048]{1,0:T(8,128)(2,1)}, u32[]{:S(2)}, u32[]{:S(2)}) collective-permute-start(bf16[32,2048]{1,0:T(8,128)(2,1)} %collective-permute-done.19), channel_id=1, source_target_pairs={{0,7},{1,0},{2,1},{3,2},{4,3},{5,4},{6,5},{7,6},{8,15},{9,8},{10,9... | collective-permute-start | bytes 393224 | tf_op jit(solution)/shard_map/ppermute | solution.py:252
  56.4 0.9 %copy-start.24 = (bf16[48,2048]{1,0:T(8,128)(2,1)}, bf16[48,2048]{1,0:T(8,128)(2,1)S(1)}, u32[]{:S(2)}) copy-start(bf16[48,2048]{1,0:T(8,128)(2,1)S(1)} %get-tuple-element.71.refs_8_) | copy-start | bytes 589828 | tf_op jit(solution)/shard_map/cond
  64.7 1.0 %copy-start = (f32[2,64,2048]{2,1,0:T(8,128)}, f32[2,64,2048]{2,1,0:T(8,128)S(1)}, u32[]{:S(2)}) copy-start(f32[2,64,2048]{2,1,0:T(8,128)S(1)} %get-tuple-element.106) | copy-start | bytes 3145732
  (4 other events, 3.1 us)

commit v4 on v3

--- a/solution.py
+++ b/solution.py
@@ -15,8 +15,8 @@
 TILE = 256
 F32 = jnp.float32
 BF16 = jnp.bfloat16
-CHUNKS = (48, 32)
-ROOM = sum(CHUNKS)
+ROOM = 80
+PARTS = 2
 
 
 def tables(length):
@@ -56,15 +56,31 @@
     return copy
 
 
-def open_kernel(xlines, shots, source_ref, target_ref, mirror_ref, live_ref, rec_hbm, table_hbm, *refs):
-    out_hbm, *packed_hbm, spec_hbm, full_ref, fast_ref, put_ref = refs[: 5 + len(CHUNKS)]
-    rec, table, spec, out, packed, table_sems, out_sems, packed_sems, sems = refs[5 + len(CHUNKS) :]
+def open_kernel(xlines, shots, source_hbm, target_hbm, mirror_hbm, live_hbm, rec_hbm, table_hbm, *refs):
+    out_hbm, *parts_hbm = refs[: 1 + 2 * PARTS]
+    lists_hbm = refs[1 + 2 * PARTS : 4 + 2 * PARTS]
+    source_ref, target_ref, mirror_ref, live_ref, rec, table, spec, out, packed, *lists = refs[4 + 2 * PARTS : -4]
+    index_sems, table_sems, out_sems, sems = refs[-4:]
     count, length = rec.shape
     quarter = length // 4
+    indices = [
+        start(source, target, index_sems.at[i])
+        for i, (source, target) in enumerate(
+            (
+                (source_hbm, source_ref),
+                (target_hbm, target_ref),
+                (mirror_hbm, mirror_ref),
+                (live_hbm, live_ref),
+            )
+        )
+    ]
     first = start(rec_hbm, rec, sems.at[0])
     half = table.shape[0] // 2
     halves = [pl.ds(i * half, half) for i in range(2)]
     coming = [start(table_hbm.at[h], table.at[h], table_sems.at[i]) for i, h in enumerate(halves)]
+    full_ref, fast_ref, put_ref = lists
+    for copy in indices:
+        copy.wait()
 
     me, line = lax.axis_index("shot"), lax.axis_index("xline")
     slots, owners = target_ref.shape
@@ -122,13 +138,13 @@
             parts[3] = jnp.where(lane == 0, sin_odd, parts[3])
         for p, part in enumerate(parts):
             spec[:, p * quarter + j * TILE : p * quarter + (j + 1) * TILE] = part.astype(BF16)
-    going = [start(spec, spec_hbm, sems.at[1])]
     for j in range(length // TILE):
         packed[:, tile_at(j)] = dot(pack, spec[:, tile_at(j)]).astype(BF16)
-    base = 0
-    for i, size in enumerate(CHUNKS):
-        going.append(start(packed.at[base : base + size], packed_hbm[i], packed_sems.at[i]))
-        base += size
+    going = [start(ref, hbm, index_sems.at[i]) for i, (ref, hbm) in enumerate(zip(lists, lists_hbm))]
+    for p in range(PARTS):
+        columns = tile_at(p, length // PARTS)
+        going.append(start(packed.at[:, columns], parts_hbm[p], sems.at[1 + p]))
+        going.append(start(spec.at[:, columns], parts_hbm[PARTS + p], sems.at[1 + PARTS + p]))
     for j in range(length // TILE):
         rows = dot(give, spec[:, tile_at(j)])
         if j * TILE == 2 * quarter:
@@ -143,47 +159,59 @@
     count, length = records.shape
     entries = source.shape[0]
     steps = length // TILE
+    lists = [
+        jax.ShapeDtypeStruct((entries, 1), jnp.int32),
+        jax.ShapeDtypeStruct((entries, 1), jnp.int32),
+        jax.ShapeDtypeStruct((count, entries), BF16),
+    ]
     return pl.pallas_call(
         functools.partial(open_kernel, xlines, shots),
-        in_specs=[VMEM] * 4 + [ANY] * 2,
-        out_specs=[ANY] * (2 + len(CHUNKS)) + [VMEM] * 3,
+        in_specs=[ANY] * 6,
+        out_specs=[ANY] * (1 + 2 * PARTS + len(lists)),
         out_shape=[
             jax.ShapeDtypeStruct((entries, length), BF16),
-            *[jax.ShapeDtypeStruct((size, length), BF16) for size in CHUNKS],
-            jax.ShapeDtypeStruct((count, length), BF16),
-            jax.ShapeDtypeStruct((entries, 1), jnp.int32),
-            jax.ShapeDtypeStruct((entries, 1), jnp.int32),
-            jax.ShapeDtypeStruct((count, entries), BF16),
+            *[jax.ShapeDtypeStruct((ROOM, length // PARTS), BF16)] * PARTS,
+            *[jax.ShapeDtypeStruct((count, length // PARTS), BF16)] * PARTS,
+            *lists,
         ],
         scratch_shapes=[
+            pltpu.VMEM(source.shape, jnp.int32),
+            pltpu.VMEM(target.shape, jnp.int32),
+            pltpu.VMEM(mirror.shape, jnp.int32),
+            pltpu.VMEM(live.shape, jnp.int32),
             pltpu.VMEM((count, length), BF16),
             pltpu.VMEM(table.shape, BF16),
             pltpu.VMEM((count, length), BF16),
             pltpu.VMEM((steps, entries, TILE), BF16),
             pltpu.VMEM((ROOM, length), BF16),
+            *[pltpu.VMEM(l.shape, l.dtype) for l in lists],
+            pltpu.SemaphoreType.DMA((4,)),
             pltpu.SemaphoreType.DMA((2,)),
             pltpu.SemaphoreType.DMA((steps,)),
-            pltpu.SemaphoreType.DMA((len(CHUNKS),)),
-            pltpu.SemaphoreType.DMA((2,)),
+            pltpu.SemaphoreType.DMA((1 + 2 * PARTS,)),
         ],
         compiler_params=PARAMS,
     )(source, target, mirror, live, records, table)
 
 
-def close_kernel(want_ref, put_ref, inverse_hbm, received_hbm, *refs):
-    *chunks, out_ref, rows, received, inverse, rows_sems, sems = refs
+def close_kernel(want_hbm, put_hbm, inverse_hbm, received_hbm, *refs):
+    *chunks, out_ref, want_ref, put_ref, rows, received, inverse, rows_sems, sems = refs
     length = inverse.shape[1]
     quarter = length // 4
-    coming, base = [], 0
+    size, columns = chunks[0].shape
+    lists = [start(want_hbm, want_ref, sems.at[0]), start(put_hbm, put_ref, sems.at[1])]
+    coming = []
     for i, chunk in enumerate(chunks):
-        size = chunk.shape[0]
-        coming.append(start(chunk, rows.at[base : base + size], rows_sems.at[i]))
-        base += size
-    other = start(received_hbm, received, sems.at[0])
+        block, part = i // PARTS, i % PARTS
+        place = rows.at[block * size : (block + 1) * size, part * columns : (part + 1) * columns]
+        coming.append(start(chunk, place, rows_sems.at[i]))
+    other = start(received_hbm, received, sems.at[2])
+    table = start(inverse_hbm, inverse, sems.at[3])
+    for copy in lists:
+        copy.wait()
     take = one_hot(want_ref[...], iota((1, rows.shape[0]), 1))
     for copy in coming:
         copy.wait()
-    pieces = [start(inverse_hbm, inverse, sems.at[1])]
     put = put_ref[...]
     count = put.shape[0]
     lane = iota((1, TILE), 1)
@@ -198,8 +226,7 @@
             b_re, b_im = received[:, re].astype(F32), received[:, im].astype(F32)
             for product in (a_re * b_re - a_im * b_im, a_re * b_im + a_im * b_re):
                 high = product.astype(BF16)
-                low = (product - high.astype(F32)).astype(BF16)
-                sums.append((dot(put, high) + dot(put, low)).astype(BF16).astype(F32))
+                sums.append(dot(put, high).astype(BF16).astype(F32))
         re, im, mirror_re, mirror_im = sums
         even_re, odd_re, even_im, odd_im = re + mirror_re, re - mirror_re, im - mirror_im, im + mirror_im
         if j == 0:
@@ -208,7 +235,7 @@
         stacks.append(
             [jnp.concatenate(pair, axis=0).astype(BF16) for pair in ((even_re, odd_re), (even_im, odd_im))]
         )
-    pieces[0].wait()
+    table.wait()
     odd = lax.rem(iota((1, TILE), 1), 2) == 1
     for c in range(length // TILE):
         acc = None
@@ -224,15 +251,17 @@
     entries, length = received.shape
     return pl.pallas_call(
         close_kernel,
-        in_specs=[VMEM] * 2 + [ANY] * (2 + len(chunks)),
+        in_specs=[ANY] * (4 + len(chunks)),
         out_specs=VMEM,
         out_shape=jax.ShapeDtypeStruct((put.shape[0], length), F32),
         scratch_shapes=[
-            pltpu.VMEM((sum(c.shape[0] for c in chunks), length), BF16),
+            pltpu.VMEM(want.shape, jnp.int32),
+            pltpu.VMEM(put.shape, BF16),
+            pltpu.VMEM((len(chunks) // PARTS * chunks[0].shape[0], length), BF16),
             pltpu.VMEM((entries, length), BF16),
             pltpu.VMEM(inverse.shape, BF16),
             pltpu.SemaphoreType.DMA((len(chunks),)),
-            pltpu.SemaphoreType.DMA((2,)),
+            pltpu.SemaphoreType.DMA((4,)),
         ],
         compiler_params=PARAMS,
     )(want, put, inverse, received, *chunks)
@@ -259,7 +288,7 @@
     xlines = lax.axis_size("xline")
     owners, _, slots = source_trace.shape
     source = source_trace.transpose(0, 2, 1).reshape(owners * slots, owners)
-    outgoing, *packed, spectra, full, fast, put = open_rows(
+    outgoing, *parts, full, fast, put = open_rows(
         source,
         target_trace[0].T,
         mirror[0].T,
@@ -272,17 +301,16 @@
     received = lax.all_to_all(
         outgoing.reshape(owners, slots, length), "shot", split_axis=0, concat_axis=0, tiled=True
     ).reshape(owners * slots, length)
-    chunks = ring(packed, xlines)
+    chunks = ring(parts[:PARTS], xlines)
     over = jnp.any(received[::slots, length // 2] != 0)
 
     def whole(received, spectra, full, fast, put, chunks):
-        parts = [spectra[: count // 2], spectra[count // 2 :]]
-        return close(full, put, inverse, received, ring(parts, xlines))
+        return close(full, put, inverse, received, ring(spectra, xlines))
 
     def short(received, spectra, full, fast, put, chunks):
         return close(fast, put, inverse, received, chunks)
 
-    predicted = lax.cond(over, whole, short, received, spectra, full, fast, put, chunks)
+    predicted = lax.cond(over, whole, short, received, parts[PARTS:], full, fast, put, chunks)
     return predicted.reshape(shot_dev, rx_local, length)
 
 

time: 66 us -> 56.6 us (0.86)
  waiting for transfers between devices: 12.8 us -> 8.58 us
  Pallas kernels: 16.4 us -> 12.5 us
  starting transfers between devices: 33.1 us -> 31.7 us
    ppermute x7, waiting for transfers between devices: 4.33 us -> 0.15 us  [ring(): above[s] = chunks[step, s] = lax.ppermute(above[s], 'xline', down)]
    pallas_call x2, Pallas kernels: 16.4 us -> 12.5 us  [the longest x1 6.55 us: open_rows(): pl.pallas_call(functools.partial(open_kernel, xlines, shots), in_specs=[A...]
    ppermute x7, starting transfers between devices: 4.12 us -> 2.11 us  [ring(): below[s] = chunks[xlines - step, s] = lax.ppermute(below[s], 'xline', up)]
  transfers between devices with their start and end apart: 15 -> 15, of which waited for: 5 -> 7; matrix products, arithmetic and copies ran while one was open for 1% -> 1% of each run, Pallas kernels for 0% -> 0%
where the time goes in v4:
time: 56.6 us; the launch traced here: 56.2 us
  starting transfers between devices  31.7 us (56%)
  Pallas kernels  12.5 us (22%)
  waiting for transfers between devices  8.58 us (15%)
  local copies, waits for them, and re-layouts  1.97 us (3%)
  between operations  0.75 us (1%)
  other arithmetic  0.65 us (1%)
    ppermute x7, starting transfers between devices, ring(): above[s] = chunks[step, s] = lax.ppermute(above[s], 'xline', down)  21.9 us
    ppermute x7, waiting for transfers between devices, ring(): below[s] = chunks[xlines - step, s] = lax.ppermute(below[s], 'xline', up)  8.43 us
    all_to_all x1, starting transfers between devices, on_device(): lax.all_to_all(outgoing.reshape(owners, slots, length), 'shot', split_axi...  7.63 us
    pallas_call x1, Pallas kernels, open_rows(): pl.pallas_call(functools.partial(open_kernel, xlines, shots), in_specs=[A...  6.55 us
    pallas_call x1, Pallas kernels, close(): pl.pallas_call(close_kernel, in_specs=[ANY] * (4 + len(chunks)), out_spec...  5.94 us
    ppermute x7, starting transfers between devices, ring(): below[s] = chunks[xlines - step, s] = lax.ppermute(below[s], 'xline', up)  2.11 us
  transfers between devices with their start and end apart: 15, of which 7 were waited for; matrix products, arithmetic and copies ran while one was open for 1% of the time, Pallas kernels for 0%

profile of v4, /device:TPU:2, one launch (start us, length us, event | category | flops | bytes accessed | tf_op | source)
XLA Modules:
  0.0 56.2 jit_solution(16108803368530253524)
XLA Ops:
  0.0 6.6 %shard_map.75 = (bf16[512,2048]{1,0:T(8,128)(2,1)}, bf16[80,1024]{1,0:T(8,128)(2,1)S(1)}, bf16[80,1024]{1,0:T(8,128)(2,1)S(1)}, bf16[128,1024]{1,0:T(8,128)(2,1)...) custom-call(s32[512,32]{1,0:T(8,128)} %bitcast.21, ...), custom_call_target="tpu_custom_call" | custom-call | tf_op jit(solution)/shard_map/pallas_call | solution.py:167
  6.6 7.6 %all-to-all-start = ((bf16[32,16,2048]{2,1,0:T(8,128)(2,1)}), bf16[32,16,2048]{2,1,0:T(8,128)(2,1)S(1)}, u32[]{:S(2)}, u32[]{:S(2)}) async-start(bf16[32,16,2048]{2,1,0:T(8,128)(2,1)} %bitcast.17), calls=%async_computation | async-start | bytes 4194304 | tf_op jit(solution)/shard_map/all_to_all | solution.py:301
  14.2 2.0 %collective-permute-start.20 = (bf16[80,1024]{1,0:T(8,128)(2,1)S(1)}, bf16[80,1024]{1,0:T(8,128)(2,1)S(1)}, u32[]{:S(2)}, u32[]{:S(2)}) collective-permute-start(bf16[80,1024]{1,0:T(8,128)(2,1)S(1)} %get-tuple-element.98), channel_id=1, source_target_pairs={{0,1},{1,2},{2,3},{3,4},{4,5},{5,6},{6,7},{7,0},{8,9},{9,10},{10,1... | collective-permute-start | bytes 491528 | tf_op jit(solution)/shard_map/ppermute | solution.py:279
  16.2 4.0 %collective-permute-start.15 = (bf16[80,1024]{1,0:T(8,128)(2,1)S(1)}, bf16[80,1024]{1,0:T(8,128)(2,1)S(1)}, u32[]{:S(2)}, u32[]{:S(2)}) collective-permute-start(bf16[80,1024]{1,0:T(8,128)(2,1)S(1)} %get-tuple-element.99), channel_id=1, source_target_pairs={{0,7},{1,0},{2,1},{3,2},{4,3},{5,4},{6,5},{7,6},{8,15},{9,8},{10,9... | collective-permute-start | bytes 491528 | tf_op jit(solution)/shard_map/ppermute | solution.py:281
  20.2 1.9 %collective-permute-start.14 = (bf16[80,1024]{1,0:T(8,128)(2,1)S(1)}, bf16[80,1024]{1,0:T(8,128)(2,1)S(1)}, u32[]{:S(2)}, u32[]{:S(2)}) collective-permute-start(bf16[80,1024]{1,0:T(8,128)(2,1)S(1)} %get-tuple-element.98), channel_id=1, source_target_pairs={{0,7},{1,0},{2,1},{3,2},{4,3},{5,4},{6,5},{7,6},{8,15},{9,8},{10,9... | collective-permute-start | bytes 491528 | tf_op jit(solution)/shard_map/ppermute | solution.py:281
  22.2 0.1 collective-permute-start.25
  22.3 2.4 %collective-permute-done.20 = bf16[80,1024]{1,0:T(8,128)(2,1)S(1)} collective-permute-done((bf16[80,1024]{1,0:T(8,128)(2,1)S(1)}, bf16[80,1024]{1,0:T(8,128)(2,1)S(1)}, u32[]{:S(2)}, u32[]{:S(2)}) %collective-permute-start.20) | collective-permute-done | bytes 163872 | tf_op jit(solution)/shard_map/ppermute | solution.py:279
  24.7 0.1 collective-permute-done.15
  24.8 3.7 %collective-permute-start.17 = (bf16[80,1024]{1,0:T(8,128)(2,1)S(1)}, bf16[80,1024]{1,0:T(8,128)(2,1)S(1)}, u32[]{:S(2)}, u32[]{:S(2)}) collective-permute-start(bf16[80,1024]{1,0:T(8,128)(2,1)S(1)} %collective-permute-done.15), channel_id=1, source_target_pairs={{0,7},{1,0},{2,1},{3,2},{4,3},{5,4},{6,5},{7,6},{8,15},{9,8},{10,9... | collective-permute-start | bytes 491528 | tf_op jit(solution)/shard_map/ppermute | solution.py:281
  28.5 2.8 %collective-permute-start.16 = (bf16[80,1024]{1,0:T(8,128)(2,1)S(1)}, bf16[80,1024]{1,0:T(8,128)(2,1)S(1)}, u32[]{:S(2)}, u32[]{:S(2)}) collective-permute-start(bf16[80,1024]{1,0:T(8,128)(2,1)S(1)} %collective-permute-done.14), channel_id=1, source_target_pairs={{0,7},{1,0},{2,1},{3,2},{4,3},{5,4},{6,5},{7,6},{8,15},{9,8},{10,9... | collective-permute-start | bytes 491528 | tf_op jit(solution)/shard_map/ppermute | solution.py:281
  31.3 1.0 %collective-permute-done.21 = bf16[80,1024]{1,0:T(8,128)(2,1)S(1)} collective-permute-done((bf16[80,1024]{1,0:T(8,128)(2,1)S(1)}, bf16[80,1024]{1,0:T(8,128)(2,1)S(1)}, u32[]{:S(2)}, u32[]{:S(2)}) %collective-permute-start.21) | collective-permute-done | bytes 163872 | tf_op jit(solution)/shard_map/ppermute | solution.py:279
  32.3 3.4 %collective-permute-start.19 = (bf16[80,1024]{1,0:T(8,128)(2,1)S(1)}, bf16[80,1024]{1,0:T(8,128)(2,1)S(1)}, u32[]{:S(2)}, u32[]{:S(2)}) collective-permute-start(bf16[80,1024]{1,0:T(8,128)(2,1)S(1)} %collective-permute-done.17), channel_id=1, source_target_pairs={{0,7},{1,0},{2,1},{3,2},{4,3},{5,4},{6,5},{7,6},{8,15},{9,8},{10,9... | collective-permute-start | bytes 491528 | tf_op jit(solution)/shard_map/ppermute | solution.py:281
  35.7 2.8 %collective-permute-start.18 = (bf16[80,1024]{1,0:T(8,128)(2,1)S(1)}, bf16[80,1024]{1,0:T(8,128)(2,1)}, u32[]{:S(2)}, u32[]{:S(2)}) collective-permute-start(bf16[80,1024]{1,0:T(8,128)(2,1)S(1)} %collective-permute-done.16), channel_id=1, source_target_pairs={{0,7},{1,0},{2,1},{3,2},{4,3},{5,4},{6,5},{7,6},{8,15},{9,8},{10,9... | collective-permute-start | bytes 491528 | tf_op jit(solution)/shard_map/ppermute | solution.py:281
  38.5 0.8 %collective-permute-done.26 = bf16[80,1024]{1,0:T(8,128)(2,1)S(1)} collective-permute-done((bf16[80,1024]{1,0:T(8,128)(2,1)S(1)}, bf16[80,1024]{1,0:T(8,128)(2,1)S(1)}, u32[]{:S(2)}, u32[]{:S(2)}) %collective-permute-start.26) | collective-permute-done | bytes 163872 | tf_op jit(solution)/shard_map/ppermute | solution.py:279
  39.3 1.8 %collective-permute-done.22 = bf16[80,1024]{1,0:T(8,128)(2,1)S(1)} collective-permute-done((bf16[80,1024]{1,0:T(8,128)(2,1)S(1)}, bf16[80,1024]{1,0:T(8,128)(2,1)S(1)}, u32[]{:S(2)}, u32[]{:S(2)}) %collective-permute-start.22) | collective-permute-done | bytes 163872 | tf_op jit(solution)/shard_map/ppermute | solution.py:279
  41.1 3.3 %collective-permute-start.24 = (bf16[80,1024]{1,0:T(8,128)(2,1)S(1)}, bf16[80,1024]{1,0:T(8,128)(2,1)}, u32[]{:S(2)}, u32[]{:S(2)}) collective-permute-start(bf16[80,1024]{1,0:T(8,128)(2,1)S(1)} %collective-permute-done.19), channel_id=1, source_target_pairs={{0,7},{1,0},{2,1},{3,2},{4,3},{5,4},{6,5},{7,6},{8,15},{9,8},{10,9... | collective-permute-start | bytes 491528 | tf_op jit(solution)/shard_map/ppermute | solution.py:281
  44.4 0.1 slice.3
  44.5 0.7 %compare_reduce_fusion = pred[]{:T(512)} fusion(bf16[32,1]{1,0:T(8,128)(2,1)S(1)} %slice.3), kind=kLoop, calls=%fused_computation | loop fusion | flops 63 | bytes 65 | tf_op jit(solution)/shard_map/reduce_or | solution.py:305
  45.8 0.7 %collective-permute-done.27 = bf16[80,1024]{1,0:T(8,128)(2,1)} collective-permute-done((bf16[80,1024]{1,0:T(8,128)(2,1)S(1)}, bf16[80,1024]{1,0:T(8,128)(2,1)}, u32[]{:S(2)}, u32[]{:S(2)}) %collective-permute-start.27) | collective-permute-done | bytes 163872 | tf_op jit(solution)/shard_map/ppermute | solution.py:279
  46.5 1.8 %collective-permute-done.23 = bf16[80,1024]{1,0:T(8,128)(2,1)} collective-permute-done((bf16[80,1024]{1,0:T(8,128)(2,1)S(1)}, bf16[80,1024]{1,0:T(8,128)(2,1)}, u32[]{:S(2)}, u32[]{:S(2)}) %collective-permute-start.23) | collective-permute-done | bytes 163872 | tf_op jit(solution)/shard_map/ppermute | solution.py:279
  48.3 6.9 %conditional.1 = (f32[2,64,2048]{2,1,0:T(8,128)S(1)}) conditional(s32[]{:T(128)} %convert_element_type.3, (s32[512,1]{1,0:T(8,128)}, bf16[128,512]{1,0:T(8,128)(2,1)S(1)}, bf16[1024,2048]{1,0:T(8,128)(2,1)}, bf16[512,2048]{1,0:T(8,128)(2,1)S(1)}, bf16[80,1024]{1,0:T(8,128)(2,1)S(1)}, /*index=5*/bf16[80,1024]{1,0:T(8,128)(2,1)S(1)}, ...), branch_computations={%region_1.0_spmd, %region_2.0_spmd} | conditional | bytes 29361088 | solution.py:313
  48.3 0.6 %copy-done.15 = bf16[80,1024]{1,0:T(8,128)(2,1)} copy-done((bf16[80,1024]{1,0:T(8,128)(2,1)}, bf16[80,1024]{1,0:T(8,128)(2,1)S(1)}, u32[]{:S(2)}) %copy-start.15) | copy-done | bytes 163864 | tf_op jit(solution)/shard_map/cond
  49.3 5.9 %branch_0_fun.1 = f32[128,2048]{1,0:T(8,128)S(1)} custom-call(s32[512,1]{1,0:T(8,128)} %get-tuple-element.61.want_hbm, bf16[128,512]{1,0:T(8,128)(2,1)S(1)} %get-tuple-element.62.put_hbm, bf16[1024,2048]{1,0:T(8,128)(2,1)} %get-tuple-element.63.inverse_hbm, bf16[512,2048]{1,0:T(8,128)(2,1)S(1)} %get-tuple-element.64.received_hbm, ...), custom_call_target="tpu_custom_call" | custom-call | tf_op jit(solution)/shard_map/cond/branch_0_fun/pallas_call | solution.py:252
  55.2 1.0 %copy-done = f32[2,64,2048]{2,1,0:T(8,128)} copy-done((f32[2,64,2048]{2,1,0:T(8,128)}, f32[2,64,2048]{2,1,0:T(8,128)S(1)}, u32[]{:S(2)}) %copy-start) | copy-done | bytes 1048600
  (37 shorter events, 0.4 us)
Async XLA Ops:
  6.6 37.9 %all-to-all-start = ((bf16[32,16,2048]{2,1,0:T(8,128)(2,1)}), bf16[32,16,2048]{2,1,0:T(8,128)(2,1)S(1)}, u32[]{:S(2)}, u32[]{:S(2)}) async-start(bf16[32,16,2048]{2,1,0:T(8,128)(2,1)} %bitcast.17), calls=%async_computation | async-start | bytes 4194304 | tf_op jit(solution)/shard_map/all_to_all | solution.py:301
  14.2 10.4 %collective-permute-start.20 = (bf16[80,1024]{1,0:T(8,128)(2,1)S(1)}, bf16[80,1024]{1,0:T(8,128)(2,1)S(1)}, u32[]{:S(2)}, u32[]{:S(2)}) collective-permute-start(bf16[80,1024]{1,0:T(8,128)(2,1)S(1)} %get-tuple-element.98), channel_id=1, source_target_pairs={{0,1},{1,2},{2,3},{3,4},{4,5},{5,6},{6,7},{7,0},{8,9},{9,10},{10,1... | collective-permute-start | bytes 491528 | tf_op jit(solution)/shard_map/ppermute | solution.py:279
  16.2 8.6 %collective-permute-start.15 = (bf16[80,1024]{1,0:T(8,128)(2,1)S(1)}, bf16[80,1024]{1,0:T(8,128)(2,1)S(1)}, u32[]{:S(2)}, u32[]{:S(2)}) collective-permute-start(bf16[80,1024]{1,0:T(8,128)(2,1)S(1)} %get-tuple-element.99), channel_id=1, source_target_pairs={{0,7},{1,0},{2,1},{3,2},{4,3},{5,4},{6,5},{7,6},{8,15},{9,8},{10,9... | collective-permute-start | bytes 491528 | tf_op jit(solution)/shard_map/ppermute | solution.py:281
  20.2 8.3 %collective-permute-start.14 = (bf16[80,1024]{1,0:T(8,128)(2,1)S(1)}, bf16[80,1024]{1,0:T(8,128)(2,1)S(1)}, u32[]{:S(2)}, u32[]{:S(2)}) collective-permute-start(bf16[80,1024]{1,0:T(8,128)(2,1)S(1)} %get-tuple-element.98), channel_id=1, source_target_pairs={{0,7},{1,0},{2,1},{3,2},{4,3},{5,4},{6,5},{7,6},{8,15},{9,8},{10,9... | collective-permute-start | bytes 491528 | tf_op jit(solution)/shard_map/ppermute | solution.py:281
  22.2 9.1 %collective-permute-start.25 = (bf16[80,1024]{1,0:T(8,128)(2,1)S(1)}, bf16[80,1024]{1,0:T(8,128)(2,1)S(1)}, u32[]{:S(2)}, u32[]{:S(2)}) collective-permute-start(bf16[80,1024]{1,0:T(8,128)(2,1)S(1)} %get-tuple-element.99), channel_id=1, source_target_pairs={{0,1},{1,2},{2,3},{3,4},{4,5},{5,6},{6,7},{7,0},{8,9},{9,10},{10,1... | collective-permute-start | bytes 491528 | tf_op jit(solution)/shard_map/ppermute | solution.py:279
  24.7 16.4 %copy-start.17 = (bf16[80,1024]{1,0:T(8,128)(2,1)}, bf16[80,1024]{1,0:T(8,128)(2,1)S(1)}, u32[]{:S(2)}) copy-start(bf16[80,1024]{1,0:T(8,128)(2,1)S(1)} %collective-permute-done.20) | copy-start | bytes 491524
  24.7 7.6 %collective-permute-start.21 = (bf16[80,1024]{1,0:T(8,128)(2,1)S(1)}, bf16[80,1024]{1,0:T(8,128)(2,1)S(1)}, u32[]{:S(2)}, u32[]{:S(2)}) collective-permute-start(bf16[80,1024]{1,0:T(8,128)(2,1)S(1)} %collective-permute-done.20), channel_id=1, source_target_pairs={{0,1},{1,2},{2,3},{3,4},{4,5},{5,6},{6,7},{7,0},{8,9},{9,10},{10,1... | collective-permute-start | bytes 491528 | tf_op jit(solution)/shard_map/ppermute | solution.py:279
  24.8 16.3 %copy-start.18 = (bf16[80,1024]{1,0:T(8,128)(2,1)}, bf16[80,1024]{1,0:T(8,128)(2,1)S(1)}, u32[]{:S(2)}) copy-start(bf16[80,1024]{1,0:T(8,128)(2,1)S(1)} %collective-permute-done.15) | copy-start | bytes 491524
  24.8 7.5 %collective-permute-start.17 = (bf16[80,1024]{1,0:T(8,128)(2,1)S(1)}, bf16[80,1024]{1,0:T(8,128)(2,1)S(1)}, u32[]{:S(2)}, u32[]{:S(2)}) collective-permute-start(bf16[80,1024]{1,0:T(8,128)(2,1)S(1)} %collective-permute-done.15), channel_id=1, source_target_pairs={{0,7},{1,0},{2,1},{3,2},{4,3},{5,4},{6,5},{7,6},{8,15},{9,8},{10,9... | collective-permute-start | bytes 491528 | tf_op jit(solution)/shard_map/ppermute | solution.py:281
  28.5 12.6 %copy-start.19 = (bf16[80,1024]{1,0:T(8,128)(2,1)}, bf16[80,1024]{1,0:T(8,128)(2,1)S(1)}, u32[]{:S(2)}) copy-start(bf16[80,1024]{1,0:T(8,128)(2,1)S(1)} %collective-permute-done.14) | copy-start | bytes 491524
  28.5 7.2 %collective-permute-start.16 = (bf16[80,1024]{1,0:T(8,128)(2,1)S(1)}, bf16[80,1024]{1,0:T(8,128)(2,1)S(1)}, u32[]{:S(2)}, u32[]{:S(2)}) collective-permute-start(bf16[80,1024]{1,0:T(8,128)(2,1)S(1)} %collective-permute-done.14), channel_id=1, source_target_pairs={{0,7},{1,0},{2,1},{3,2},{4,3},{5,4},{6,5},{7,6},{8,15},{9,8},{10,9... | collective-permute-start | bytes 491528 | tf_op jit(solution)/shard_map/ppermute | solution.py:281
  31.3 9.8 %copy-start.20 = (bf16[80,1024]{1,0:T(8,128)(2,1)}, bf16[80,1024]{1,0:T(8,128)(2,1)S(1)}, u32[]{:S(2)}) copy-start(bf16[80,1024]{1,0:T(8,128)(2,1)S(1)} %collective-permute-done.25) | copy-start | bytes 491524
  31.3 8.0 %collective-permute-start.26 = (bf16[80,1024]{1,0:T(8,128)(2,1)S(1)}, bf16[80,1024]{1,0:T(8,128)(2,1)S(1)}, u32[]{:S(2)}, u32[]{:S(2)}) collective-permute-start(bf16[80,1024]{1,0:T(8,128)(2,1)S(1)} %collective-permute-done.25), channel_id=1, source_target_pairs={{0,1},{1,2},{2,3},{3,4},{4,5},{5,6},{6,7},{7,0},{8,9},{9,10},{10,1... | collective-permute-start | bytes 491528 | tf_op jit(solution)/shard_map/ppermute | solution.py:279
  32.3 8.8 %copy-start.21 = (bf16[80,1024]{1,0:T(8,128)(2,1)}, bf16[80,1024]{1,0:T(8,128)(2,1)S(1)}, u32[]{:S(2)}) copy-start(bf16[80,1024]{1,0:T(8,128)(2,1)S(1)} %collective-permute-done.21) | copy-start | bytes 491524
  32.3 8.8 %collective-permute-start.22 = (bf16[80,1024]{1,0:T(8,128)(2,1)S(1)}, bf16[80,1024]{1,0:T(8,128)(2,1)S(1)}, u32[]{:S(2)}, u32[]{:S(2)}) collective-permute-start(bf16[80,1024]{1,0:T(8,128)(2,1)S(1)} %collective-permute-done.21), channel_id=1, source_target_pairs={{0,1},{1,2},{2,3},{3,4},{4,5},{5,6},{6,7},{7,0},{8,9},{9,10},{10,1... | collective-permute-start | bytes 491528 | tf_op jit(solution)/shard_map/ppermute | solution.py:279
  32.3 8.8 %copy-start.22 = (bf16[80,1024]{1,0:T(8,128)(2,1)}, bf16[80,1024]{1,0:T(8,128)(2,1)S(1)}, u32[]{:S(2)}) copy-start(bf16[80,1024]{1,0:T(8,128)(2,1)S(1)} %collective-permute-done.17) | copy-start | bytes 491524
  32.3 8.8 %collective-permute-start.19 = (bf16[80,1024]{1,0:T(8,128)(2,1)S(1)}, bf16[80,1024]{1,0:T(8,128)(2,1)S(1)}, u32[]{:S(2)}, u32[]{:S(2)}) collective-permute-start(bf16[80,1024]{1,0:T(8,128)(2,1)S(1)} %collective-permute-done.17), channel_id=1, source_target_pairs={{0,7},{1,0},{2,1},{3,2},{4,3},{5,4},{6,5},{7,6},{8,15},{9,8},{10,9... | collective-permute-start | bytes 491528 | tf_op jit(solution)/shard_map/ppermute | solution.py:281
  35.7 10.1 %collective-permute-start.18 = (bf16[80,1024]{1,0:T(8,128)(2,1)S(1)}, bf16[80,1024]{1,0:T(8,128)(2,1)}, u32[]{:S(2)}, u32[]{:S(2)}) collective-permute-start(bf16[80,1024]{1,0:T(8,128)(2,1)S(1)} %collective-permute-done.16), channel_id=1, source_target_pairs={{0,7},{1,0},{2,1},{3,2},{4,3},{5,4},{6,5},{7,6},{8,15},{9,8},{10,9... | collective-permute-start | bytes 491528 | tf_op jit(solution)/shard_map/ppermute | solution.py:281
  39.3 7.2 %collective-permute-start.27 = (bf16[80,1024]{1,0:T(8,128)(2,1)S(1)}, bf16[80,1024]{1,0:T(8,128)(2,1)}, u32[]{:S(2)}, u32[]{:S(2)}) collective-permute-start(bf16[80,1024]{1,0:T(8,128)(2,1)S(1)} %collective-permute-done.26), channel_id=1, source_target_pairs={{0,1},{1,2},{2,3},{3,4},{4,5},{5,6},{6,7},{7,0},{8,9},{9,10},{10,1... | collective-permute-start | bytes 491528 | tf_op jit(solution)/shard_map/ppermute | solution.py:279
  41.1 7.2 %collective-permute-start.23 = (bf16[80,1024]{1,0:T(8,128)(2,1)S(1)}, bf16[80,1024]{1,0:T(8,128)(2,1)}, u32[]{:S(2)}, u32[]{:S(2)}) collective-permute-start(bf16[80,1024]{1,0:T(8,128)(2,1)S(1)} %collective-permute-done.22), channel_id=1, source_target_pairs={{0,1},{1,2},{2,3},{3,4},{4,5},{5,6},{6,7},{7,0},{8,9},{9,10},{10,1... | collective-permute-start | bytes 491528 | tf_op jit(solution)/shard_map/ppermute | solution.py:279
  41.1 7.2 %collective-permute-start.24 = (bf16[80,1024]{1,0:T(8,128)(2,1)S(1)}, bf16[80,1024]{1,0:T(8,128)(2,1)}, u32[]{:S(2)}, u32[]{:S(2)}) collective-permute-start(bf16[80,1024]{1,0:T(8,128)(2,1)S(1)} %collective-permute-done.19), channel_id=1, source_target_pairs={{0,7},{1,0},{2,1},{3,2},{4,3},{5,4},{6,5},{7,6},{8,15},{9,8},{10,9... | collective-permute-start | bytes 491528 | tf_op jit(solution)/shard_map/ppermute | solution.py:281
  48.3 0.9 %copy-start.25 = (bf16[80,1024]{1,0:T(8,128)(2,1)}, bf16[80,1024]{1,0:T(8,128)(2,1)S(1)}, u32[]{:S(2)}) copy-start(bf16[80,1024]{1,0:T(8,128)(2,1)S(1)} %get-tuple-element.75.refs_10_) | copy-start | bytes 491524 | tf_op jit(solution)/shard_map/cond
  48.3 0.9 %copy-start.26 = (bf16[80,1024]{1,0:T(8,128)(2,1)}, bf16[80,1024]{1,0:T(8,128)(2,1)S(1)}, u32[]{:S(2)}) copy-start(bf16[80,1024]{1,0:T(8,128)(2,1)S(1)} %get-tuple-element.72.refs_7_) | copy-start | bytes 491524 | tf_op jit(solution)/shard_map/cond
  55.2 1.0 %copy-start = (f32[2,64,2048]{2,1,0:T(8,128)}, f32[2,64,2048]{2,1,0:T(8,128)S(1)}, u32[]{:S(2)}) copy-start(f32[2,64,2048]{2,1,0:T(8,128)S(1)} %get-tuple-element.109) | copy-start | bytes 3145732
  (4 other events, 3.0 us)

commit v5 on v4

--- a/solution.py
+++ b/solution.py
@@ -15,7 +15,7 @@
 TILE = 256
 F32 = jnp.float32
 BF16 = jnp.bfloat16
-ROOM = 80
+ROOM = 64
 PARTS = 2
 
 

time: 56.6 us -> 52.8 us (0.933)
  waiting for transfers between devices: 8.58 us -> 6.15 us
  starting transfers between devices: 31.7 us -> 30.8 us
  Pallas kernels: 12.5 us -> 11.8 us
    ppermute x7, waiting for transfers between devices: 8.43 us -> 5.37 us  [ring(): below[s] = chunks[xlines - step, s] = lax.ppermute(below[s], 'xline', up)]
    ppermute x7, starting transfers between devices: 21.9 us -> 20.8 us  [ring(): above[s] = chunks[step, s] = lax.ppermute(above[s], 'xline', down)]
    pallas_call x1, Pallas kernels: 5.94 us -> 5.23 us  [close(): pl.pallas_call(close_kernel, in_specs=[ANY] * (4 + len(chunks)), out_spec...]
    ppermute x7, waiting for transfers between devices: 0.15 us -> 0.78 us  [ring(): above[s] = chunks[step, s] = lax.ppermute(above[s], 'xline', down)]
  transfers between devices with their start and end apart: 15 -> 15, of which waited for: 7 -> 8; matrix products, arithmetic and copies ran while one was open for 1% -> 1% of each run, Pallas kernels for 0% -> 0%
where the time goes in v5:
time: 52.8 us; the launch traced here: 52.2 us
  starting transfers between devices  30.8 us (58%)
  Pallas kernels  11.8 us (22%)
  waiting for transfers between devices  6.15 us (12%)
  local copies, waits for them, and re-layouts  1.98 us (4%)
  between operations  0.71 us (1%)
  other arithmetic  0.7 us (1%)
    ppermute x7, starting transfers between devices, ring(): above[s] = chunks[step, s] = lax.ppermute(above[s], 'xline', down)  20.8 us
    all_to_all x1, starting transfers between devices, on_device(): lax.all_to_all(outgoing.reshape(owners, slots, length), 'shot', split_axi...  7.63 us
    pallas_call x1, Pallas kernels, open_rows(): pl.pallas_call(functools.partial(open_kernel, xlines, shots), in_specs=[A...  6.53 us
    ppermute x7, waiting for transfers between devices, ring(): below[s] = chunks[xlines - step, s] = lax.ppermute(below[s], 'xline', up)  5.37 us
    pallas_call x1, Pallas kernels, close(): pl.pallas_call(close_kernel, in_specs=[ANY] * (4 + len(chunks)), out_spec...  5.23 us
    ppermute x7, starting transfers between devices, ring(): below[s] = chunks[xlines - step, s] = lax.ppermute(below[s], 'xline', up)  2.36 us
  transfers between devices with their start and end apart: 15, of which 8 were waited for; matrix products, arithmetic and copies ran while one was open for 1% of the time, Pallas kernels for 0%

profile of v5, /device:TPU:2, one launch (start us, length us, event | category | flops | bytes accessed | tf_op | source)
XLA Modules:
  0.0 52.2 jit_solution(5218449095248486910)
XLA Ops:
  0.0 6.5 %shard_map.75 = (bf16[512,2048]{1,0:T(8,128)(2,1)}, bf16[64,1024]{1,0:T(8,128)(2,1)S(1)}, bf16[64,1024]{1,0:T(8,128)(2,1)S(1)}, bf16[128,1024]{1,0:T(8,128)(2,1)...) custom-call(s32[512,32]{1,0:T(8,128)} %bitcast.21, ...), custom_call_target="tpu_custom_call" | custom-call | tf_op jit(solution)/shard_map/pallas_call | solution.py:167
  6.5 7.6 %all-to-all-start = ((bf16[32,16,2048]{2,1,0:T(8,128)(2,1)}), bf16[32,16,2048]{2,1,0:T(8,128)(2,1)S(1)}, u32[]{:S(2)}, u32[]{:S(2)}) async-start(bf16[32,16,2048]{2,1,0:T(8,128)(2,1)} %bitcast.17), calls=%async_computation | async-start | bytes 4194304 | tf_op jit(solution)/shard_map/all_to_all | solution.py:301
  14.2 2.0 %collective-permute-start.20 = (bf16[64,1024]{1,0:T(8,128)(2,1)S(1)}, bf16[64,1024]{1,0:T(8,128)(2,1)S(1)}, u32[]{:S(2)}, u32[]{:S(2)}) collective-permute-start(bf16[64,1024]{1,0:T(8,128)(2,1)S(1)} %get-tuple-element.98), channel_id=1, source_target_pairs={{0,1},{1,2},{2,3},{3,4},{4,5},{5,6},{6,7},{7,0},{8,9},{9,10},{10,1... | collective-permute-start | bytes 393224 | tf_op jit(solution)/shard_map/ppermute | solution.py:279
  16.2 4.0 %collective-permute-start.15 = (bf16[64,1024]{1,0:T(8,128)(2,1)S(1)}, bf16[64,1024]{1,0:T(8,128)(2,1)S(1)}, u32[]{:S(2)}, u32[]{:S(2)}) collective-permute-start(bf16[64,1024]{1,0:T(8,128)(2,1)S(1)} %get-tuple-element.99), channel_id=1, source_target_pairs={{0,7},{1,0},{2,1},{3,2},{4,3},{5,4},{6,5},{7,6},{8,15},{9,8},{10,9... | collective-permute-start | bytes 393224 | tf_op jit(solution)/shard_map/ppermute | solution.py:281
  20.2 1.9 %collective-permute-start.14 = (bf16[64,1024]{1,0:T(8,128)(2,1)S(1)}, bf16[64,1024]{1,0:T(8,128)(2,1)S(1)}, u32[]{:S(2)}, u32[]{:S(2)}) collective-permute-start(bf16[64,1024]{1,0:T(8,128)(2,1)S(1)} %get-tuple-element.98), channel_id=1, source_target_pairs={{0,7},{1,0},{2,1},{3,2},{4,3},{5,4},{6,5},{7,6},{8,15},{9,8},{10,9... | collective-permute-start | bytes 393224 | tf_op jit(solution)/shard_map/ppermute | solution.py:281
  22.2 1.7 %collective-permute-done.20 = bf16[64,1024]{1,0:T(8,128)(2,1)S(1)} collective-permute-done((bf16[64,1024]{1,0:T(8,128)(2,1)S(1)}, bf16[64,1024]{1,0:T(8,128)(2,1)S(1)}, u32[]{:S(2)}, u32[]{:S(2)}) %collective-permute-start.20) | collective-permute-done | bytes 131104 | tf_op jit(solution)/shard_map/ppermute | solution.py:279
  23.9 0.1 collective-permute-done.15
  24.1 3.7 %collective-permute-start.17 = (bf16[64,1024]{1,0:T(8,128)(2,1)S(1)}, bf16[64,1024]{1,0:T(8,128)(2,1)S(1)}, u32[]{:S(2)}, u32[]{:S(2)}) collective-permute-start(bf16[64,1024]{1,0:T(8,128)(2,1)S(1)} %collective-permute-done.15), channel_id=1, source_target_pairs={{0,7},{1,0},{2,1},{3,2},{4,3},{5,4},{6,5},{7,6},{8,15},{9,8},{10,9... | collective-permute-start | bytes 393224 | tf_op jit(solution)/shard_map/ppermute | solution.py:281
  27.8 2.0 %collective-permute-start.16 = (bf16[64,1024]{1,0:T(8,128)(2,1)S(1)}, bf16[64,1024]{1,0:T(8,128)(2,1)S(1)}, u32[]{:S(2)}, u32[]{:S(2)}) collective-permute-start(bf16[64,1024]{1,0:T(8,128)(2,1)S(1)} %collective-permute-done.14), channel_id=1, source_target_pairs={{0,7},{1,0},{2,1},{3,2},{4,3},{5,4},{6,5},{7,6},{8,15},{9,8},{10,9... | collective-permute-start | bytes 393224 | tf_op jit(solution)/shard_map/ppermute | solution.py:281
  29.8 1.3 %collective-permute-done.21 = bf16[64,1024]{1,0:T(8,128)(2,1)S(1)} collective-permute-done((bf16[64,1024]{1,0:T(8,128)(2,1)S(1)}, bf16[64,1024]{1,0:T(8,128)(2,1)S(1)}, u32[]{:S(2)}, u32[]{:S(2)}) %collective-permute-start.21) | collective-permute-done | bytes 131104 | tf_op jit(solution)/shard_map/ppermute | solution.py:279
  31.1 0.2 collective-permute-done.17
  31.4 3.7 %collective-permute-start.19 = (bf16[64,1024]{1,0:T(8,128)(2,1)S(1)}, bf16[64,1024]{1,0:T(8,128)(2,1)S(1)}, u32[]{:S(2)}, u32[]{:S(2)}) collective-permute-start(bf16[64,1024]{1,0:T(8,128)(2,1)S(1)} %collective-permute-done.17), channel_id=1, source_target_pairs={{0,7},{1,0},{2,1},{3,2},{4,3},{5,4},{6,5},{7,6},{8,15},{9,8},{10,9... | collective-permute-start | bytes 393224 | tf_op jit(solution)/shard_map/ppermute | solution.py:281
  35.1 1.7 %collective-permute-start.18 = (bf16[64,1024]{1,0:T(8,128)(2,1)S(1)}, bf16[64,1024]{1,0:T(8,128)(2,1)S(1)}, u32[]{:S(2)}, u32[]{:S(2)}) collective-permute-start(bf16[64,1024]{1,0:T(8,128)(2,1)S(1)} %collective-permute-done.16), channel_id=1, source_target_pairs={{0,7},{1,0},{2,1},{3,2},{4,3},{5,4},{6,5},{7,6},{8,15},{9,8},{10,9... | collective-permute-start | bytes 393224 | tf_op jit(solution)/shard_map/ppermute | solution.py:281
  36.7 0.1 collective-permute-done.26
  36.8 0.3 collective-permute-start.27
  37.1 1.1 %collective-permute-done.22 = bf16[64,1024]{1,0:T(8,128)(2,1)S(1)} collective-permute-done((bf16[64,1024]{1,0:T(8,128)(2,1)S(1)}, bf16[64,1024]{1,0:T(8,128)(2,1)S(1)}, u32[]{:S(2)}, u32[]{:S(2)}) %collective-permute-start.22) | collective-permute-done | bytes 131104 | tf_op jit(solution)/shard_map/ppermute | solution.py:279
  38.3 0.4 collective-permute-done.19
  38.7 3.8 %collective-permute-start.24 = (bf16[64,1024]{1,0:T(8,128)(2,1)S(1)}, bf16[64,1024]{1,0:T(8,128)(2,1)}, u32[]{:S(2)}, u32[]{:S(2)}) collective-permute-start(bf16[64,1024]{1,0:T(8,128)(2,1)S(1)} %collective-permute-done.19), channel_id=1, source_target_pairs={{0,7},{1,0},{2,1},{3,2},{4,3},{5,4},{6,5},{7,6},{8,15},{9,8},{10,9... | collective-permute-start | bytes 393224 | tf_op jit(solution)/shard_map/ppermute | solution.py:281
  42.5 0.7 %compare_reduce_fusion = pred[]{:T(512)} fusion(bf16[32,1]{1,0:T(8,128)(2,1)S(1)} %slice.3), kind=kLoop, calls=%fused_computation | loop fusion | flops 63 | bytes 65 | tf_op jit(solution)/shard_map/reduce_or | solution.py:305
  43.9 1.1 %collective-permute-done.23 = bf16[64,1024]{1,0:T(8,128)(2,1)} collective-permute-done((bf16[64,1024]{1,0:T(8,128)(2,1)S(1)}, bf16[64,1024]{1,0:T(8,128)(2,1)}, u32[]{:S(2)}, u32[]{:S(2)}) %collective-permute-start.23) | collective-permute-done | bytes 131104 | tf_op jit(solution)/shard_map/ppermute | solution.py:279
  45.0 6.2 %conditional.1 = (f32[2,64,2048]{2,1,0:T(8,128)S(1)}) conditional(s32[]{:T(128)} %convert_element_type.3, (s32[512,1]{1,0:T(8,128)}, bf16[128,512]{1,0:T(8,128)(2,1)S(1)}, bf16[1024,2048]{1,0:T(8,128)(2,1)}, bf16[512,2048]{1,0:T(8,128)(2,1)S(1)}, bf16[64,1024]{1,0:T(8,128)(2,1)S(1)}, /*index=5*/bf16[64,1024]{1,0:T(8,128)(2,1)S(1)}, ...), branch_computations={%region_1.0_spmd, %region_2.0_spmd} | conditional | bytes 29361088 | solution.py:313
  45.1 0.6 %copy-done.15 = bf16[64,1024]{1,0:T(8,128)(2,1)} copy-done((bf16[64,1024]{1,0:T(8,128)(2,1)}, bf16[64,1024]{1,0:T(8,128)(2,1)S(1)}, u32[]{:S(2)}) %copy-start.15) | copy-done | bytes 131096 | tf_op jit(solution)/shard_map/cond
  46.0 5.2 %branch_0_fun.1 = f32[128,2048]{1,0:T(8,128)S(1)} custom-call(s32[512,1]{1,0:T(8,128)} %get-tuple-element.61.want_hbm, bf16[128,512]{1,0:T(8,128)(2,1)S(1)} %get-tuple-element.62.put_hbm, bf16[1024,2048]{1,0:T(8,128)(2,1)} %get-tuple-element.63.inverse_hbm, bf16[512,2048]{1,0:T(8,128)(2,1)S(1)} %get-tuple-element.64.received_hbm, ...), custom_call_target="tpu_custom_call" | custom-call | tf_op jit(solution)/shard_map/cond/branch_0_fun/pallas_call | solution.py:252
  51.2 1.0 %copy-done = f32[2,64,2048]{2,1,0:T(8,128)} copy-done((f32[2,64,2048]{2,1,0:T(8,128)}, f32[2,64,2048]{2,1,0:T(8,128)S(1)}, u32[]{:S(2)}) %copy-start) | copy-done | bytes 1048600
  (41 shorter events, 0.6 us)
Async XLA Ops:
  6.5 35.9 %all-to-all-start = ((bf16[32,16,2048]{2,1,0:T(8,128)(2,1)}), bf16[32,16,2048]{2,1,0:T(8,128)(2,1)S(1)}, u32[]{:S(2)}, u32[]{:S(2)}) async-start(bf16[32,16,2048]{2,1,0:T(8,128)(2,1)} %bitcast.17), calls=%async_computation | async-start | bytes 4194304 | tf_op jit(solution)/shard_map/all_to_all | solution.py:301
  14.2 9.7 %collective-permute-start.20 = (bf16[64,1024]{1,0:T(8,128)(2,1)S(1)}, bf16[64,1024]{1,0:T(8,128)(2,1)S(1)}, u32[]{:S(2)}, u32[]{:S(2)}) collective-permute-start(bf16[64,1024]{1,0:T(8,128)(2,1)S(1)} %get-tuple-element.98), channel_id=1, source_target_pairs={{0,1},{1,2},{2,3},{3,4},{4,5},{5,6},{6,7},{7,0},{8,9},{9,10},{10,1... | collective-permute-start | bytes 393224 | tf_op jit(solution)/shard_map/ppermute | solution.py:279
  16.2 7.9 %collective-permute-start.15 = (bf16[64,1024]{1,0:T(8,128)(2,1)S(1)}, bf16[64,1024]{1,0:T(8,128)(2,1)S(1)}, u32[]{:S(2)}, u32[]{:S(2)}) collective-permute-start(bf16[64,1024]{1,0:T(8,128)(2,1)S(1)} %get-tuple-element.99), channel_id=1, source_target_pairs={{0,7},{1,0},{2,1},{3,2},{4,3},{5,4},{6,5},{7,6},{8,15},{9,8},{10,9... | collective-permute-start | bytes 393224 | tf_op jit(solution)/shard_map/ppermute | solution.py:281
  20.2 7.6 %collective-permute-start.14 = (bf16[64,1024]{1,0:T(8,128)(2,1)S(1)}, bf16[64,1024]{1,0:T(8,128)(2,1)S(1)}, u32[]{:S(2)}, u32[]{:S(2)}) collective-permute-start(bf16[64,1024]{1,0:T(8,128)(2,1)S(1)} %get-tuple-element.98), channel_id=1, source_target_pairs={{0,7},{1,0},{2,1},{3,2},{4,3},{5,4},{6,5},{7,6},{8,15},{9,8},{10,9... | collective-permute-start | bytes 393224 | tf_op jit(solution)/shard_map/ppermute | solution.py:281
  22.1 7.6 %collective-permute-start.25 = (bf16[64,1024]{1,0:T(8,128)(2,1)S(1)}, bf16[64,1024]{1,0:T(8,128)(2,1)S(1)}, u32[]{:S(2)}, u32[]{:S(2)}) collective-permute-start(bf16[64,1024]{1,0:T(8,128)(2,1)S(1)} %get-tuple-element.99), channel_id=1, source_target_pairs={{0,1},{1,2},{2,3},{3,4},{4,5},{5,6},{6,7},{7,0},{8,9},{9,10},{10,1... | collective-permute-start | bytes 393224 | tf_op jit(solution)/shard_map/ppermute | solution.py:279
  23.9 14.7 %copy-start.17 = (bf16[64,1024]{1,0:T(8,128)(2,1)}, bf16[64,1024]{1,0:T(8,128)(2,1)S(1)}, u32[]{:S(2)}) copy-start(bf16[64,1024]{1,0:T(8,128)(2,1)S(1)} %collective-permute-done.20) | copy-start | bytes 393220
  23.9 7.2 %collective-permute-start.21 = (bf16[64,1024]{1,0:T(8,128)(2,1)S(1)}, bf16[64,1024]{1,0:T(8,128)(2,1)S(1)}, u32[]{:S(2)}, u32[]{:S(2)}) collective-permute-start(bf16[64,1024]{1,0:T(8,128)(2,1)S(1)} %collective-permute-done.20), channel_id=1, source_target_pairs={{0,1},{1,2},{2,3},{3,4},{4,5},{5,6},{6,7},{7,0},{8,9},{9,10},{10,1... | collective-permute-start | bytes 393224 | tf_op jit(solution)/shard_map/ppermute | solution.py:279
  24.1 14.6 %copy-start.18 = (bf16[64,1024]{1,0:T(8,128)(2,1)}, bf16[64,1024]{1,0:T(8,128)(2,1)S(1)}, u32[]{:S(2)}) copy-start(bf16[64,1024]{1,0:T(8,128)(2,1)S(1)} %collective-permute-done.15) | copy-start | bytes 393220
  24.1 7.3 %collective-permute-start.17 = (bf16[64,1024]{1,0:T(8,128)(2,1)S(1)}, bf16[64,1024]{1,0:T(8,128)(2,1)S(1)}, u32[]{:S(2)}, u32[]{:S(2)}) collective-permute-start(bf16[64,1024]{1,0:T(8,128)(2,1)S(1)} %collective-permute-done.15), channel_id=1, source_target_pairs={{0,7},{1,0},{2,1},{3,2},{4,3},{5,4},{6,5},{7,6},{8,15},{9,8},{10,9... | collective-permute-start | bytes 393224 | tf_op jit(solution)/shard_map/ppermute | solution.py:281
  27.8 10.9 %copy-start.19 = (bf16[64,1024]{1,0:T(8,128)(2,1)}, bf16[64,1024]{1,0:T(8,128)(2,1)S(1)}, u32[]{:S(2)}) copy-start(bf16[64,1024]{1,0:T(8,128)(2,1)S(1)} %collective-permute-done.14) | copy-start | bytes 393220
  27.8 7.3 %collective-permute-start.16 = (bf16[64,1024]{1,0:T(8,128)(2,1)S(1)}, bf16[64,1024]{1,0:T(8,128)(2,1)S(1)}, u32[]{:S(2)}, u32[]{:S(2)}) collective-permute-start(bf16[64,1024]{1,0:T(8,128)(2,1)S(1)} %collective-permute-done.14), channel_id=1, source_target_pairs={{0,7},{1,0},{2,1},{3,2},{4,3},{5,4},{6,5},{7,6},{8,15},{9,8},{10,9... | collective-permute-start | bytes 393224 | tf_op jit(solution)/shard_map/ppermute | solution.py:281
  29.8 8.9 %copy-start.20 = (bf16[64,1024]{1,0:T(8,128)(2,1)}, bf16[64,1024]{1,0:T(8,128)(2,1)S(1)}, u32[]{:S(2)}) copy-start(bf16[64,1024]{1,0:T(8,128)(2,1)S(1)} %collective-permute-done.25) | copy-start | bytes 393220
  29.8 7.1 %collective-permute-start.26 = (bf16[64,1024]{1,0:T(8,128)(2,1)S(1)}, bf16[64,1024]{1,0:T(8,128)(2,1)S(1)}, u32[]{:S(2)}, u32[]{:S(2)}) collective-permute-start(bf16[64,1024]{1,0:T(8,128)(2,1)S(1)} %collective-permute-done.25), channel_id=1, source_target_pairs={{0,1},{1,2},{2,3},{3,4},{4,5},{5,6},{6,7},{7,0},{8,9},{9,10},{10,1... | collective-permute-start | bytes 393224 | tf_op jit(solution)/shard_map/ppermute | solution.py:279
  31.1 7.5 %copy-start.21 = (bf16[64,1024]{1,0:T(8,128)(2,1)}, bf16[64,1024]{1,0:T(8,128)(2,1)S(1)}, u32[]{:S(2)}) copy-start(bf16[64,1024]{1,0:T(8,128)(2,1)S(1)} %collective-permute-done.21) | copy-start | bytes 393220
  31.1 7.1 %collective-permute-start.22 = (bf16[64,1024]{1,0:T(8,128)(2,1)S(1)}, bf16[64,1024]{1,0:T(8,128)(2,1)S(1)}, u32[]{:S(2)}, u32[]{:S(2)}) collective-permute-start(bf16[64,1024]{1,0:T(8,128)(2,1)S(1)} %collective-permute-done.21), channel_id=1, source_target_pairs={{0,1},{1,2},{2,3},{3,4},{4,5},{5,6},{6,7},{7,0},{8,9},{9,10},{10,1... | collective-permute-start | bytes 393224 | tf_op jit(solution)/shard_map/ppermute | solution.py:279
  31.4 7.3 %copy-start.22 = (bf16[64,1024]{1,0:T(8,128)(2,1)}, bf16[64,1024]{1,0:T(8,128)(2,1)S(1)}, u32[]{:S(2)}) copy-start(bf16[64,1024]{1,0:T(8,128)(2,1)S(1)} %collective-permute-done.17) | copy-start | bytes 393220
  31.4 7.3 %collective-permute-start.19 = (bf16[64,1024]{1,0:T(8,128)(2,1)S(1)}, bf16[64,1024]{1,0:T(8,128)(2,1)S(1)}, u32[]{:S(2)}, u32[]{:S(2)}) collective-permute-start(bf16[64,1024]{1,0:T(8,128)(2,1)S(1)} %collective-permute-done.17), channel_id=1, source_target_pairs={{0,7},{1,0},{2,1},{3,2},{4,3},{5,4},{6,5},{7,6},{8,15},{9,8},{10,9... | collective-permute-start | bytes 393224 | tf_op jit(solution)/shard_map/ppermute | solution.py:281
  35.1 8.8 %collective-permute-start.18 = (bf16[64,1024]{1,0:T(8,128)(2,1)S(1)}, bf16[64,1024]{1,0:T(8,128)(2,1)S(1)}, u32[]{:S(2)}, u32[]{:S(2)}) collective-permute-start(bf16[64,1024]{1,0:T(8,128)(2,1)S(1)} %collective-permute-done.16), channel_id=1, source_target_pairs={{0,7},{1,0},{2,1},{3,2},{4,3},{5,4},{6,5},{7,6},{8,15},{9,8},{10,9... | collective-permute-start | bytes 393224 | tf_op jit(solution)/shard_map/ppermute | solution.py:281
  36.8 7.0 %collective-permute-start.27 = (bf16[64,1024]{1,0:T(8,128)(2,1)S(1)}, bf16[64,1024]{1,0:T(8,128)(2,1)S(1)}, u32[]{:S(2)}, u32[]{:S(2)}) collective-permute-start(bf16[64,1024]{1,0:T(8,128)(2,1)S(1)} %collective-permute-done.26), channel_id=1, source_target_pairs={{0,1},{1,2},{2,3},{3,4},{4,5},{5,6},{6,7},{7,0},{8,9},{9,10},{10,1... | collective-permute-start | bytes 393224 | tf_op jit(solution)/shard_map/ppermute | solution.py:279
  38.2 6.7 %collective-permute-start.23 = (bf16[64,1024]{1,0:T(8,128)(2,1)S(1)}, bf16[64,1024]{1,0:T(8,128)(2,1)}, u32[]{:S(2)}, u32[]{:S(2)}) collective-permute-start(bf16[64,1024]{1,0:T(8,128)(2,1)S(1)} %collective-permute-done.22), channel_id=1, source_target_pairs={{0,1},{1,2},{2,3},{3,4},{4,5},{5,6},{6,7},{7,0},{8,9},{9,10},{10,1... | collective-permute-start | bytes 393224 | tf_op jit(solution)/shard_map/ppermute | solution.py:279
  38.7 6.3 %collective-permute-start.24 = (bf16[64,1024]{1,0:T(8,128)(2,1)S(1)}, bf16[64,1024]{1,0:T(8,128)(2,1)}, u32[]{:S(2)}, u32[]{:S(2)}) collective-permute-start(bf16[64,1024]{1,0:T(8,128)(2,1)S(1)} %collective-permute-done.19), channel_id=1, source_target_pairs={{0,7},{1,0},{2,1},{3,2},{4,3},{5,4},{6,5},{7,6},{8,15},{9,8},{10,9... | collective-permute-start | bytes 393224 | tf_op jit(solution)/shard_map/ppermute | solution.py:281
  45.0 0.9 %copy-start.27 = (bf16[64,1024]{1,0:T(8,128)(2,1)}, bf16[64,1024]{1,0:T(8,128)(2,1)S(1)}, u32[]{:S(2)}) copy-start(bf16[64,1024]{1,0:T(8,128)(2,1)S(1)} %get-tuple-element.71.refs_6_) | copy-start | bytes 393220 | tf_op jit(solution)/shard_map/cond
  45.0 0.9 %copy-start.28 = (bf16[64,1024]{1,0:T(8,128)(2,1)}, bf16[64,1024]{1,0:T(8,128)(2,1)S(1)}, u32[]{:S(2)}) copy-start(bf16[64,1024]{1,0:T(8,128)(2,1)S(1)} %get-tuple-element.76.refs_11_) | copy-start | bytes 393220 | tf_op jit(solution)/shard_map/cond
  51.2 1.0 %copy-start = (f32[2,64,2048]{2,1,0:T(8,128)}, f32[2,64,2048]{2,1,0:T(8,128)S(1)}, u32[]{:S(2)}) copy-start(f32[2,64,2048]{2,1,0:T(8,128)S(1)} %get-tuple-element.109) | copy-start | bytes 3145732
  (6 other events, 4.5 us)

commit v6 on v5

--- a/solution.py
+++ b/solution.py
@@ -275,10 +275,10 @@
     chunks = {(0, s): part for s, part in enumerate(parts)}
     for step in range(1, half + 1):
         for s in range(2):
+            if step < half or s == 1:
+                above[s] = chunks[step, s] = lax.ppermute(above[s], "xline", down)
             if step < half or s == 0:
                 below[s] = chunks[xlines - step, s] = lax.ppermute(below[s], "xline", up)
-            if step < half or s == 1:
-                above[s] = chunks[step, s] = lax.ppermute(above[s], "xline", down)
     return [chunks[o, s] for o in range(xlines) for s in range(2)]
 
 

time: 52.8 us -> 52.8 us (level)
  no operation moved by 1% of the time
where the time goes in v6:
time: 52.8 us; the launch traced here: 52.2 us
  starting transfers between devices  30.8 us (58%)
  Pallas kernels  11.8 us (22%)
  waiting for transfers between devices  6.15 us (12%)
  local copies, waits for them, and re-layouts  1.98 us (4%)
  between operations  0.71 us (1%)
  other arithmetic  0.7 us (1%)
    ppermute x7, starting transfers between devices, ring(): above[s] = chunks[step, s] = lax.ppermute(above[s], 'xline', down)  20.8 us
    all_to_all x1, starting transfers between devices, on_device(): lax.all_to_all(outgoing.reshape(owners, slots, length), 'shot', split_axi...  7.63 us
    pallas_call x1, Pallas kernels, open_rows(): pl.pallas_call(functools.partial(open_kernel, xlines, shots), in_specs=[A...  6.53 us
    ppermute x7, waiting for transfers between devices, ring(): below[s] = chunks[xlines - step, s] = lax.ppermute(below[s], 'xline', up)  5.37 us
    pallas_call x1, Pallas kernels, close(): pl.pallas_call(close_kernel, in_specs=[ANY] * (4 + len(chunks)), out_spec...  5.23 us
    ppermute x7, starting transfers between devices, ring(): below[s] = chunks[xlines - step, s] = lax.ppermute(below[s], 'xline', up)  2.36 us
  transfers between devices with their start and end apart: 15, of which 8 were waited for; matrix products, arithmetic and copies ran while one was open for 1% of the time, Pallas kernels for 0%

profile of v6, /device:TPU:2, one launch (start us, length us, event | category | flops | bytes accessed | tf_op | source)
XLA Modules:
  0.0 52.2 jit_solution(5218449095248486910)
XLA Ops:
  0.0 6.5 %shard_map.75 = (bf16[512,2048]{1,0:T(8,128)(2,1)}, bf16[64,1024]{1,0:T(8,128)(2,1)S(1)}, bf16[64,1024]{1,0:T(8,128)(2,1)S(1)}, bf16[128,1024]{1,0:T(8,128)(2,1)...) custom-call(s32[512,32]{1,0:T(8,128)} %bitcast.21, ...), custom_call_target="tpu_custom_call" | custom-call | tf_op jit(solution)/shard_map/pallas_call | solution.py:167
  6.5 7.6 %all-to-all-start = ((bf16[32,16,2048]{2,1,0:T(8,128)(2,1)}), bf16[32,16,2048]{2,1,0:T(8,128)(2,1)S(1)}, u32[]{:S(2)}, u32[]{:S(2)}) async-start(bf16[32,16,2048]{2,1,0:T(8,128)(2,1)} %bitcast.17), calls=%async_computation | async-start | bytes 4194304 | tf_op jit(solution)/shard_map/all_to_all | solution.py:301
  14.2 2.0 %collective-permute-start.20 = (bf16[64,1024]{1,0:T(8,128)(2,1)S(1)}, bf16[64,1024]{1,0:T(8,128)(2,1)S(1)}, u32[]{:S(2)}, u32[]{:S(2)}) collective-permute-start(bf16[64,1024]{1,0:T(8,128)(2,1)S(1)} %get-tuple-element.98), channel_id=1, source_target_pairs={{0,1},{1,2},{2,3},{3,4},{4,5},{5,6},{6,7},{7,0},{8,9},{9,10},{10,1... | collective-permute-start | bytes 393224 | tf_op jit(solution)/shard_map/ppermute | solution.py:281
  16.2 4.0 %collective-permute-start.15 = (bf16[64,1024]{1,0:T(8,128)(2,1)S(1)}, bf16[64,1024]{1,0:T(8,128)(2,1)S(1)}, u32[]{:S(2)}, u32[]{:S(2)}) collective-permute-start(bf16[64,1024]{1,0:T(8,128)(2,1)S(1)} %get-tuple-element.99), channel_id=1, source_target_pairs={{0,7},{1,0},{2,1},{3,2},{4,3},{5,4},{6,5},{7,6},{8,15},{9,8},{10,9... | collective-permute-start | bytes 393224 | tf_op jit(solution)/shard_map/ppermute | solution.py:279
  20.2 1.9 %collective-permute-start.14 = (bf16[64,1024]{1,0:T(8,128)(2,1)S(1)}, bf16[64,1024]{1,0:T(8,128)(2,1)S(1)}, u32[]{:S(2)}, u32[]{:S(2)}) collective-permute-start(bf16[64,1024]{1,0:T(8,128)(2,1)S(1)} %get-tuple-element.98), channel_id=1, source_target_pairs={{0,7},{1,0},{2,1},{3,2},{4,3},{5,4},{6,5},{7,6},{8,15},{9,8},{10,9... | collective-permute-start | bytes 393224 | tf_op jit(solution)/shard_map/ppermute | solution.py:279
  22.2 1.7 %collective-permute-done.20 = bf16[64,1024]{1,0:T(8,128)(2,1)S(1)} collective-permute-done((bf16[64,1024]{1,0:T(8,128)(2,1)S(1)}, bf16[64,1024]{1,0:T(8,128)(2,1)S(1)}, u32[]{:S(2)}, u32[]{:S(2)}) %collective-permute-start.20) | collective-permute-done | bytes 131104 | tf_op jit(solution)/shard_map/ppermute | solution.py:281
  23.9 0.1 collective-permute-done.15
  24.1 3.7 %collective-permute-start.17 = (bf16[64,1024]{1,0:T(8,128)(2,1)S(1)}, bf16[64,1024]{1,0:T(8,128)(2,1)S(1)}, u32[]{:S(2)}, u32[]{:S(2)}) collective-permute-start(bf16[64,1024]{1,0:T(8,128)(2,1)S(1)} %collective-permute-done.15), channel_id=1, source_target_pairs={{0,7},{1,0},{2,1},{3,2},{4,3},{5,4},{6,5},{7,6},{8,15},{9,8},{10,9... | collective-permute-start | bytes 393224 | tf_op jit(solution)/shard_map/ppermute | solution.py:279
  27.8 2.0 %collective-permute-start.16 = (bf16[64,1024]{1,0:T(8,128)(2,1)S(1)}, bf16[64,1024]{1,0:T(8,128)(2,1)S(1)}, u32[]{:S(2)}, u32[]{:S(2)}) collective-permute-start(bf16[64,1024]{1,0:T(8,128)(2,1)S(1)} %collective-permute-done.14), channel_id=1, source_target_pairs={{0,7},{1,0},{2,1},{3,2},{4,3},{5,4},{6,5},{7,6},{8,15},{9,8},{10,9... | collective-permute-start | bytes 393224 | tf_op jit(solution)/shard_map/ppermute | solution.py:279
  29.8 1.3 %collective-permute-done.21 = bf16[64,1024]{1,0:T(8,128)(2,1)S(1)} collective-permute-done((bf16[64,1024]{1,0:T(8,128)(2,1)S(1)}, bf16[64,1024]{1,0:T(8,128)(2,1)S(1)}, u32[]{:S(2)}, u32[]{:S(2)}) %collective-permute-start.21) | collective-permute-done | bytes 131104 | tf_op jit(solution)/shard_map/ppermute | solution.py:281
  31.1 0.2 collective-permute-done.17
  31.4 3.7 %collective-permute-start.19 = (bf16[64,1024]{1,0:T(8,128)(2,1)S(1)}, bf16[64,1024]{1,0:T(8,128)(2,1)S(1)}, u32[]{:S(2)}, u32[]{:S(2)}) collective-permute-start(bf16[64,1024]{1,0:T(8,128)(2,1)S(1)} %collective-permute-done.17), channel_id=1, source_target_pairs={{0,7},{1,0},{2,1},{3,2},{4,3},{5,4},{6,5},{7,6},{8,15},{9,8},{10,9... | collective-permute-start | bytes 393224 | tf_op jit(solution)/shard_map/ppermute | solution.py:279
  35.1 1.7 %collective-permute-start.18 = (bf16[64,1024]{1,0:T(8,128)(2,1)S(1)}, bf16[64,1024]{1,0:T(8,128)(2,1)S(1)}, u32[]{:S(2)}, u32[]{:S(2)}) collective-permute-start(bf16[64,1024]{1,0:T(8,128)(2,1)S(1)} %collective-permute-done.16), channel_id=1, source_target_pairs={{0,7},{1,0},{2,1},{3,2},{4,3},{5,4},{6,5},{7,6},{8,15},{9,8},{10,9... | collective-permute-start | bytes 393224 | tf_op jit(solution)/shard_map/ppermute | solution.py:279
  36.7 0.1 collective-permute-done.26
  36.8 0.3 collective-permute-start.27
  37.1 1.1 %collective-permute-done.22 = bf16[64,1024]{1,0:T(8,128)(2,1)S(1)} collective-permute-done((bf16[64,1024]{1,0:T(8,128)(2,1)S(1)}, bf16[64,1024]{1,0:T(8,128)(2,1)S(1)}, u32[]{:S(2)}, u32[]{:S(2)}) %collective-permute-start.22) | collective-permute-done | bytes 131104 | tf_op jit(solution)/shard_map/ppermute | solution.py:281
  38.3 0.4 collective-permute-done.19
  38.7 3.8 %collective-permute-start.24 = (bf16[64,1024]{1,0:T(8,128)(2,1)S(1)}, bf16[64,1024]{1,0:T(8,128)(2,1)}, u32[]{:S(2)}, u32[]{:S(2)}) collective-permute-start(bf16[64,1024]{1,0:T(8,128)(2,1)S(1)} %collective-permute-done.19), channel_id=1, source_target_pairs={{0,7},{1,0},{2,1},{3,2},{4,3},{5,4},{6,5},{7,6},{8,15},{9,8},{10,9... | collective-permute-start | bytes 393224 | tf_op jit(solution)/shard_map/ppermute | solution.py:279
  42.5 0.7 %compare_reduce_fusion = pred[]{:T(512)} fusion(bf16[32,1]{1,0:T(8,128)(2,1)S(1)} %slice.3), kind=kLoop, calls=%fused_computation | loop fusion | flops 63 | bytes 65 | tf_op jit(solution)/shard_map/reduce_or | solution.py:305
  43.9 1.1 %collective-permute-done.23 = bf16[64,1024]{1,0:T(8,128)(2,1)} collective-permute-done((bf16[64,1024]{1,0:T(8,128)(2,1)S(1)}, bf16[64,1024]{1,0:T(8,128)(2,1)}, u32[]{:S(2)}, u32[]{:S(2)}) %collective-permute-start.23) | collective-permute-done | bytes 131104 | tf_op jit(solution)/shard_map/ppermute | solution.py:281
  45.0 6.2 %conditional.1 = (f32[2,64,2048]{2,1,0:T(8,128)S(1)}) conditional(s32[]{:T(128)} %convert_element_type.3, (s32[512,1]{1,0:T(8,128)}, bf16[128,512]{1,0:T(8,128)(2,1)S(1)}, bf16[1024,2048]{1,0:T(8,128)(2,1)}, bf16[512,2048]{1,0:T(8,128)(2,1)S(1)}, bf16[64,1024]{1,0:T(8,128)(2,1)S(1)}, /*index=5*/bf16[64,1024]{1,0:T(8,128)(2,1)S(1)}, ...), branch_computations={%region_1.0_spmd, %region_2.0_spmd} | conditional | bytes 29361088 | solution.py:313
  45.1 0.6 %copy-done.15 = bf16[64,1024]{1,0:T(8,128)(2,1)} copy-done((bf16[64,1024]{1,0:T(8,128)(2,1)}, bf16[64,1024]{1,0:T(8,128)(2,1)S(1)}, u32[]{:S(2)}) %copy-start.15) | copy-done | bytes 131096 | tf_op jit(solution)/shard_map/cond
  46.0 5.2 %branch_0_fun.1 = f32[128,2048]{1,0:T(8,128)S(1)} custom-call(s32[512,1]{1,0:T(8,128)} %get-tuple-element.61.want_hbm, bf16[128,512]{1,0:T(8,128)(2,1)S(1)} %get-tuple-element.62.put_hbm, bf16[1024,2048]{1,0:T(8,128)(2,1)} %get-tuple-element.63.inverse_hbm, bf16[512,2048]{1,0:T(8,128)(2,1)S(1)} %get-tuple-element.64.received_hbm, ...), custom_call_target="tpu_custom_call" | custom-call | tf_op jit(solution)/shard_map/cond/branch_0_fun/pallas_call | solution.py:252
  51.2 1.0 %copy-done = f32[2,64,2048]{2,1,0:T(8,128)} copy-done((f32[2,64,2048]{2,1,0:T(8,128)}, f32[2,64,2048]{2,1,0:T(8,128)S(1)}, u32[]{:S(2)}) %copy-start) | copy-done | bytes 1048600
  (41 shorter events, 0.6 us)
Async XLA Ops:
  6.5 35.9 %all-to-all-start = ((bf16[32,16,2048]{2,1,0:T(8,128)(2,1)}), bf16[32,16,2048]{2,1,0:T(8,128)(2,1)S(1)}, u32[]{:S(2)}, u32[]{:S(2)}) async-start(bf16[32,16,2048]{2,1,0:T(8,128)(2,1)} %bitcast.17), calls=%async_computation | async-start | bytes 4194304 | tf_op jit(solution)/shard_map/all_to_all | solution.py:301
  14.2 9.7 %collective-permute-start.20 = (bf16[64,1024]{1,0:T(8,128)(2,1)S(1)}, bf16[64,1024]{1,0:T(8,128)(2,1)S(1)}, u32[]{:S(2)}, u32[]{:S(2)}) collective-permute-start(bf16[64,1024]{1,0:T(8,128)(2,1)S(1)} %get-tuple-element.98), channel_id=1, source_target_pairs={{0,1},{1,2},{2,3},{3,4},{4,5},{5,6},{6,7},{7,0},{8,9},{9,10},{10,1... | collective-permute-start | bytes 393224 | tf_op jit(solution)/shard_map/ppermute | solution.py:281
  16.2 7.9 %collective-permute-start.15 = (bf16[64,1024]{1,0:T(8,128)(2,1)S(1)}, bf16[64,1024]{1,0:T(8,128)(2,1)S(1)}, u32[]{:S(2)}, u32[]{:S(2)}) collective-permute-start(bf16[64,1024]{1,0:T(8,128)(2,1)S(1)} %get-tuple-element.99), channel_id=1, source_target_pairs={{0,7},{1,0},{2,1},{3,2},{4,3},{5,4},{6,5},{7,6},{8,15},{9,8},{10,9... | collective-permute-start | bytes 393224 | tf_op jit(solution)/shard_map/ppermute | solution.py:279
  20.2 7.6 %collective-permute-start.14 = (bf16[64,1024]{1,0:T(8,128)(2,1)S(1)}, bf16[64,1024]{1,0:T(8,128)(2,1)S(1)}, u32[]{:S(2)}, u32[]{:S(2)}) collective-permute-start(bf16[64,1024]{1,0:T(8,128)(2,1)S(1)} %get-tuple-element.98), channel_id=1, source_target_pairs={{0,7},{1,0},{2,1},{3,2},{4,3},{5,4},{6,5},{7,6},{8,15},{9,8},{10,9... | collective-permute-start | bytes 393224 | tf_op jit(solution)/shard_map/ppermute | solution.py:279
  22.1 7.6 %collective-permute-start.25 = (bf16[64,1024]{1,0:T(8,128)(2,1)S(1)}, bf16[64,1024]{1,0:T(8,128)(2,1)S(1)}, u32[]{:S(2)}, u32[]{:S(2)}) collective-permute-start(bf16[64,1024]{1,0:T(8,128)(2,1)S(1)} %get-tuple-element.99), channel_id=1, source_target_pairs={{0,1},{1,2},{2,3},{3,4},{4,5},{5,6},{6,7},{7,0},{8,9},{9,10},{10,1... | collective-permute-start | bytes 393224 | tf_op jit(solution)/shard_map/ppermute | solution.py:281
  23.9 14.7 %copy-start.17 = (bf16[64,1024]{1,0:T(8,128)(2,1)}, bf16[64,1024]{1,0:T(8,128)(2,1)S(1)}, u32[]{:S(2)}) copy-start(bf16[64,1024]{1,0:T(8,128)(2,1)S(1)} %collective-permute-done.20) | copy-start | bytes 393220
  23.9 7.2 %collective-permute-start.21 = (bf16[64,1024]{1,0:T(8,128)(2,1)S(1)}, bf16[64,1024]{1,0:T(8,128)(2,1)S(1)}, u32[]{:S(2)}, u32[]{:S(2)}) collective-permute-start(bf16[64,1024]{1,0:T(8,128)(2,1)S(1)} %collective-permute-done.20), channel_id=1, source_target_pairs={{0,1},{1,2},{2,3},{3,4},{4,5},{5,6},{6,7},{7,0},{8,9},{9,10},{10,1... | collective-permute-start | bytes 393224 | tf_op jit(solution)/shard_map/ppermute | solution.py:281
  24.1 14.6 %copy-start.18 = (bf16[64,1024]{1,0:T(8,128)(2,1)}, bf16[64,1024]{1,0:T(8,128)(2,1)S(1)}, u32[]{:S(2)}) copy-start(bf16[64,1024]{1,0:T(8,128)(2,1)S(1)} %collective-permute-done.15) | copy-start | bytes 393220
  24.1 7.3 %collective-permute-start.17 = (bf16[64,1024]{1,0:T(8,128)(2,1)S(1)}, bf16[64,1024]{1,0:T(8,128)(2,1)S(1)}, u32[]{:S(2)}, u32[]{:S(2)}) collective-permute-start(bf16[64,1024]{1,0:T(8,128)(2,1)S(1)} %collective-permute-done.15), channel_id=1, source_target_pairs={{0,7},{1,0},{2,1},{3,2},{4,3},{5,4},{6,5},{7,6},{8,15},{9,8},{10,9... | collective-permute-start | bytes 393224 | tf_op jit(solution)/shard_map/ppermute | solution.py:279
  27.8 10.9 %copy-start.19 = (bf16[64,1024]{1,0:T(8,128)(2,1)}, bf16[64,1024]{1,0:T(8,128)(2,1)S(1)}, u32[]{:S(2)}) copy-start(bf16[64,1024]{1,0:T(8,128)(2,1)S(1)} %collective-permute-done.14) | copy-start | bytes 393220
  27.8 7.3 %collective-permute-start.16 = (bf16[64,1024]{1,0:T(8,128)(2,1)S(1)}, bf16[64,1024]{1,0:T(8,128)(2,1)S(1)}, u32[]{:S(2)}, u32[]{:S(2)}) collective-permute-start(bf16[64,1024]{1,0:T(8,128)(2,1)S(1)} %collective-permute-done.14), channel_id=1, source_target_pairs={{0,7},{1,0},{2,1},{3,2},{4,3},{5,4},{6,5},{7,6},{8,15},{9,8},{10,9... | collective-permute-start | bytes 393224 | tf_op jit(solution)/shard_map/ppermute | solution.py:279
  29.8 8.9 %copy-start.20 = (bf16[64,1024]{1,0:T(8,128)(2,1)}, bf16[64,1024]{1,0:T(8,128)(2,1)S(1)}, u32[]{:S(2)}) copy-start(bf16[64,1024]{1,0:T(8,128)(2,1)S(1)} %collective-permute-done.25) | copy-start | bytes 393220
  29.8 7.1 %collective-permute-start.26 = (bf16[64,1024]{1,0:T(8,128)(2,1)S(1)}, bf16[64,1024]{1,0:T(8,128)(2,1)S(1)}, u32[]{:S(2)}, u32[]{:S(2)}) collective-permute-start(bf16[64,1024]{1,0:T(8,128)(2,1)S(1)} %collective-permute-done.25), channel_id=1, source_target_pairs={{0,1},{1,2},{2,3},{3,4},{4,5},{5,6},{6,7},{7,0},{8,9},{9,10},{10,1... | collective-permute-start | bytes 393224 | tf_op jit(solution)/shard_map/ppermute | solution.py:281
  31.1 7.5 %copy-start.21 = (bf16[64,1024]{1,0:T(8,128)(2,1)}, bf16[64,1024]{1,0:T(8,128)(2,1)S(1)}, u32[]{:S(2)}) copy-start(bf16[64,1024]{1,0:T(8,128)(2,1)S(1)} %collective-permute-done.21) | copy-start | bytes 393220
  31.1 7.1 %collective-permute-start.22 = (bf16[64,1024]{1,0:T(8,128)(2,1)S(1)}, bf16[64,1024]{1,0:T(8,128)(2,1)S(1)}, u32[]{:S(2)}, u32[]{:S(2)}) collective-permute-start(bf16[64,1024]{1,0:T(8,128)(2,1)S(1)} %collective-permute-done.21), channel_id=1, source_target_pairs={{0,1},{1,2},{2,3},{3,4},{4,5},{5,6},{6,7},{7,0},{8,9},{9,10},{10,1... | collective-permute-start | bytes 393224 | tf_op jit(solution)/shard_map/ppermute | solution.py:281
  31.4 7.3 %copy-start.22 = (bf16[64,1024]{1,0:T(8,128)(2,1)}, bf16[64,1024]{1,0:T(8,128)(2,1)S(1)}, u32[]{:S(2)}) copy-start(bf16[64,1024]{1,0:T(8,128)(2,1)S(1)} %collective-permute-done.17) | copy-start | bytes 393220
  31.4 7.3 %collective-permute-start.19 = (bf16[64,1024]{1,0:T(8,128)(2,1)S(1)}, bf16[64,1024]{1,0:T(8,128)(2,1)S(1)}, u32[]{:S(2)}, u32[]{:S(2)}) collective-permute-start(bf16[64,1024]{1,0:T(8,128)(2,1)S(1)} %collective-permute-done.17), channel_id=1, source_target_pairs={{0,7},{1,0},{2,1},{3,2},{4,3},{5,4},{6,5},{7,6},{8,15},{9,8},{10,9... | collective-permute-start | bytes 393224 | tf_op jit(solution)/shard_map/ppermute | solution.py:279
  35.1 8.8 %collective-permute-start.18 = (bf16[64,1024]{1,0:T(8,128)(2,1)S(1)}, bf16[64,1024]{1,0:T(8,128)(2,1)S(1)}, u32[]{:S(2)}, u32[]{:S(2)}) collective-permute-start(bf16[64,1024]{1,0:T(8,128)(2,1)S(1)} %collective-permute-done.16), channel_id=1, source_target_pairs={{0,7},{1,0},{2,1},{3,2},{4,3},{5,4},{6,5},{7,6},{8,15},{9,8},{10,9... | collective-permute-start | bytes 393224 | tf_op jit(solution)/shard_map/ppermute | solution.py:279
  36.8 7.0 %collective-permute-start.27 = (bf16[64,1024]{1,0:T(8,128)(2,1)S(1)}, bf16[64,1024]{1,0:T(8,128)(2,1)S(1)}, u32[]{:S(2)}, u32[]{:S(2)}) collective-permute-start(bf16[64,1024]{1,0:T(8,128)(2,1)S(1)} %collective-permute-done.26), channel_id=1, source_target_pairs={{0,1},{1,2},{2,3},{3,4},{4,5},{5,6},{6,7},{7,0},{8,9},{9,10},{10,1... | collective-permute-start | bytes 393224 | tf_op jit(solution)/shard_map/ppermute | solution.py:281
  38.2 6.7 %collective-permute-start.23 = (bf16[64,1024]{1,0:T(8,128)(2,1)S(1)}, bf16[64,1024]{1,0:T(8,128)(2,1)}, u32[]{:S(2)}, u32[]{:S(2)}) collective-permute-start(bf16[64,1024]{1,0:T(8,128)(2,1)S(1)} %collective-permute-done.22), channel_id=1, source_target_pairs={{0,1},{1,2},{2,3},{3,4},{4,5},{5,6},{6,7},{7,0},{8,9},{9,10},{10,1... | collective-permute-start | bytes 393224 | tf_op jit(solution)/shard_map/ppermute | solution.py:281
  38.7 6.3 %collective-permute-start.24 = (bf16[64,1024]{1,0:T(8,128)(2,1)S(1)}, bf16[64,1024]{1,0:T(8,128)(2,1)}, u32[]{:S(2)}, u32[]{:S(2)}) collective-permute-start(bf16[64,1024]{1,0:T(8,128)(2,1)S(1)} %collective-permute-done.19), channel_id=1, source_target_pairs={{0,7},{1,0},{2,1},{3,2},{4,3},{5,4},{6,5},{7,6},{8,15},{9,8},{10,9... | collective-permute-start | bytes 393224 | tf_op jit(solution)/shard_map/ppermute | solution.py:279
  45.0 0.9 %copy-start.27 = (bf16[64,1024]{1,0:T(8,128)(2,1)}, bf16[64,1024]{1,0:T(8,128)(2,1)S(1)}, u32[]{:S(2)}) copy-start(bf16[64,1024]{1,0:T(8,128)(2,1)S(1)} %get-tuple-element.71.refs_6_) | copy-start | bytes 393220 | tf_op jit(solution)/shard_map/cond
  45.0 0.9 %copy-start.28 = (bf16[64,1024]{1,0:T(8,128)(2,1)}, bf16[64,1024]{1,0:T(8,128)(2,1)S(1)}, u32[]{:S(2)}) copy-start(bf16[64,1024]{1,0:T(8,128)(2,1)S(1)} %get-tuple-element.76.refs_11_) | copy-start | bytes 393220 | tf_op jit(solution)/shard_map/cond
  51.2 1.0 %copy-start = (f32[2,64,2048]{2,1,0:T(8,128)}, f32[2,64,2048]{2,1,0:T(8,128)S(1)}, u32[]{:S(2)}) copy-start(f32[2,64,2048]{2,1,0:T(8,128)S(1)} %get-tuple-element.109) | copy-start | bytes 3145732
  (6 other events, 4.5 us)
